TPU v7x, 32 devices: a whole 2x2x4 slice. The times are simulated.
32 devices in a mesh: frame: 4 (over y, x), seq: 8 (over z, core).
Axes of the slice: x: 2, y: 2, z: 4, core: 2. Of those that a mesh axis runs over, the one named last changes fastest.
Arguments:
- vid_q: bfloat16 [4, 256, 2048], P('frame', 'seq'), may hold values from -6 to 6
- vid_k: bfloat16 [4, 256, 2048], P('frame', 'seq'), may hold values from -6 to 6
- vid_v: bfloat16 [4, 256, 2048], P('frame', 'seq'), may hold values from -6 to 6
- vid_dout: bfloat16 [4, 256, 2048], P('frame', 'seq'), may hold values from -6 to 6
- aud_q: bfloat16 [4, 768, 2048], P('frame', 'seq'), may hold values from -6 to 6
- aud_k: bfloat16 [4, 768, 2048], P('frame', 'seq'), may hold values from -6 to 6
- aud_v: bfloat16 [4, 768, 2048], P('frame', 'seq'), may hold values from -6 to 6
- aud_dout: bfloat16 [4, 768, 2048], P('frame', 'seq'), may hold values from -6 to 6
- aud_len: int32 [4, 8], replicated, may hold values from 32 to 96, as said below
- match: int32 [4], replicated, may hold values from 0 to 3, each once
Outputs:
- d_vid_q: bfloat16 [4, 256, 2048], P('frame', 'seq')
- d_vid_k: bfloat16 [4, 256, 2048], P('frame', 'seq')
- d_vid_v: bfloat16 [4, 256, 2048], P('frame', 'seq')
- d_aud_q: bfloat16 [4, 768, 2048], P('frame', 'seq')
- d_aud_k: bfloat16 [4, 768, 2048], P('frame', 'seq')
- d_aud_v: bfloat16 [4, 768, 2048], P('frame', 'seq')
Inputs may be any that keep to these rules, and one draw needn't show every extreme that they name: `aud_len`: every entry is a whole multiple of 32; in every frame group one time block has 96 live slots and another has 32. match names every frame group once.
All inputs are finite; a program needn't handle non-finite values.
Results may differ from a plain program's by a relative error of at most 0.012.
The roundings to bfloat16 on the way count: a program that leaves them out, or rounds other values in their place, can miss the bound.
Values may be sent and summed in bfloat16 or wider, within the bound.
A program may use at most 64 MiB of HBM per device.

v0:
```python
import jax
import jax.numpy as jnp
from jax import lax
from jax.sharding import PartitionSpec as P

HD = 128
BAND = 2


NEG_BIG = -1e30


def from_behind(x, axis, by):
    peers = lax.axis_size(axis)
    pairs = [(i, i + by) for i in range(peers) if 0 <= i + by < peers]
    return lax.ppermute(x, axis, pairs)


def query_side(queries, key_rows, val_rows, grad_out, key_mask):
    factor = HD ** (-0.5)
    scores = (
        jnp.einsum("fhqd,fhkd->fhqk", queries, key_rows, preferred_element_type=jnp.float32)
        * factor
    )
    scores = jnp.where(key_mask[:, None, None, :], scores, NEG_BIG)
    largest = jnp.max(scores, axis=-1, keepdims=True)
    exponent = jnp.exp(scores - largest)
    totals = jnp.sum(exponent, axis=-1, keepdims=True)
    weights = exponent / totals
    weights_half = weights.astype(jnp.bfloat16)
    output = jnp.einsum(
        "fhqk,fhkd->fhqd", weights_half, val_rows, preferred_element_type=jnp.float32
    )
    deltas = jnp.sum(grad_out.astype(jnp.float32) * output, axis=-1, keepdims=True)
    grad_weights = jnp.einsum(
        "fhqd,fhkd->fhqk", grad_out, val_rows, preferred_element_type=jnp.float32
    )
    grad_scores = (weights * (grad_weights - deltas)).astype(jnp.bfloat16)
    grad_query = (
        jnp.einsum("fhqk,fhkd->fhqd", grad_scores, key_rows, preferred_element_type=jnp.float32)
        * factor
    )
    return (grad_query, weights_half, grad_scores, largest[..., 0], totals[..., 0], deltas[..., 0])


def shards(vid_q, vid_k, vid_v, vid_dout, aud_q, aud_k, aud_v, aud_dout, aud_len, match):
    frames = lax.axis_size("frame")
    seq_count = lax.axis_size("seq")
    here = lax.axis_index("seq")
    moved = (
        lax.all_to_all(vid_q, "frame", split_axis=2, concat_axis=0, tiled=True),
        lax.all_to_all(vid_k, "frame", split_axis=2, concat_axis=0, tiled=True),
        lax.all_to_all(vid_v, "frame", split_axis=2, concat_axis=0, tiled=True),
        lax.all_to_all(vid_dout, "frame", split_axis=2, concat_axis=0, tiled=True),
        lax.all_to_all(aud_q, "frame", split_axis=2, concat_axis=0, tiled=True),
        lax.all_to_all(aud_k, "frame", split_axis=2, concat_axis=0, tiled=True),
        lax.all_to_all(aud_v, "frame", split_axis=2, concat_axis=0, tiled=True),
        lax.all_to_all(aud_dout, "frame", split_axis=2, concat_axis=0, tiled=True),
    )
    order = jnp.arange(frames, dtype=jnp.int32)
    inverse = jnp.sum(jnp.where(match[None, :] == order[:, None], order[None, :], 0), axis=1)
    video_query, video_key, video_value, video_grad = (moved[0], moved[1], moved[2], moved[3])
    audio_query = jnp.take(moved[4], match, axis=0)
    audio_key = jnp.take(moved[5], match, axis=0)
    audio_value = jnp.take(moved[6], match, axis=0)
    audio_grad = jnp.take(moved[7], match, axis=0)
    lengths = jnp.take(aud_len, match, axis=0)
    video_rows = video_query.shape[1]
    audio_rows = audio_query.shape[1]
    width_here = video_query.shape[2]
    heads_here = width_here // HD
    slots = lax.broadcasted_iota(jnp.int32, (frames, audio_rows), 1)

    def inside(offset):
        target = here + offset
        return (target >= 0) & (target < seq_count)

    def audio_mask(offset):
        column = lax.dynamic_index_in_dim(
            lengths, jnp.clip(here + offset, 0, seq_count - 1), 1, keepdims=True
        )
        return (slots < column) & inside(offset)

    def video_mask(offset):
        return jnp.broadcast_to(inside(offset), (frames, video_rows))

    def split(array):
        shaped = array.reshape(array.shape[:-1] + (heads_here, HD))
        return jnp.moveaxis(shaped, -2, -3)

    def joined(array):
        moved_back = jnp.moveaxis(array, -3, -2)
        return moved_back.reshape(moved_back.shape[:-2] + (width_here,))

    offsets = list(range(-BAND, BAND + 1))
    audio_grad = jnp.where(audio_mask(0)[:, :, None], audio_grad, jnp.zeros((), jnp.bfloat16))
    audio_keys_mask = jnp.concatenate([audio_mask(offset) for offset in offsets], axis=1)
    video_keys_mask = jnp.concatenate([video_mask(offset) for offset in offsets], axis=1)
    factor = HD ** (-0.5)
    packed = jnp.concatenate(
        [jnp.stack([video_key, video_value]), jnp.stack([audio_key, audio_value])], axis=2
    )
    nearby = []
    for offset in offsets:
        if offset == 0:
            nearby.append(packed)
        else:
            nearby.append(from_behind(packed, "seq", -offset))
    video_window = jnp.concatenate([member[:, :, :video_rows] for member in nearby], axis=2)
    audio_window = jnp.concatenate([member[:, :, video_rows:] for member in nearby], axis=2)
    video_side = query_side(
        split(video_query),
        split(audio_window[0]),
        split(audio_window[1]),
        split(video_grad),
        audio_keys_mask,
    )
    audio_side = query_side(
        split(audio_query),
        split(video_window[0]),
        split(video_window[1]),
        split(audio_grad),
        video_keys_mask,
    )
    grad_vq = joined(video_side[0])
    grad_aq = joined(audio_side[0])
    audio_key_terms = (
        jnp.einsum(
            "fhqk,fhqd->fhkd", video_side[2], split(video_query), preferred_element_type=jnp.float32
        )
        * factor
    )
    audio_value_terms = jnp.einsum(
        "fhqk,fhqd->fhkd", video_side[1], split(video_grad), preferred_element_type=jnp.float32
    )
    video_key_terms = (
        jnp.einsum(
            "fhqk,fhqd->fhkd", audio_side[2], split(audio_query), preferred_element_type=jnp.float32
        )
        * factor
    )
    video_value_terms = jnp.einsum(
        "fhqk,fhqd->fhkd", audio_side[1], split(audio_grad), preferred_element_type=jnp.float32
    )
    video_terms = jnp.stack(
        [
            joined(video_key_terms).astype(jnp.bfloat16),
            joined(video_value_terms).astype(jnp.bfloat16),
        ]
    )
    audio_terms = jnp.stack(
        [
            joined(audio_key_terms).astype(jnp.bfloat16),
            joined(audio_value_terms).astype(jnp.bfloat16),
        ]
    )
    summed = jnp.zeros((2, frames, video_rows + audio_rows, width_here), jnp.float32)
    for position, offset in enumerate(offsets):
        piece = jnp.concatenate(
            [
                video_terms[:, :, position * video_rows : (position + 1) * video_rows],
                audio_terms[:, :, position * audio_rows : (position + 1) * audio_rows],
            ],
            axis=2,
        )
        if offset == 0:
            summed = summed + piece.astype(jnp.float32)
        else:
            summed = summed + from_behind(piece, "seq", offset).astype(jnp.float32)
    grad_vk = summed[0, :, :video_rows]
    grad_vv = summed[1, :, :video_rows]
    grad_ak = summed[0, :, video_rows:]
    grad_av = summed[1, :, video_rows:]
    grad_aq = jnp.take(grad_aq, inverse, axis=0)
    grad_ak = jnp.take(grad_ak, inverse, axis=0)
    grad_av = jnp.take(grad_av, inverse, axis=0)
    returned = (
        lax.all_to_all(
            grad_vq.astype(jnp.bfloat16), "frame", split_axis=0, concat_axis=2, tiled=True
        ),
        lax.all_to_all(
            grad_vk.astype(jnp.bfloat16), "frame", split_axis=0, concat_axis=2, tiled=True
        ),
        lax.all_to_all(
            grad_vv.astype(jnp.bfloat16), "frame", split_axis=0, concat_axis=2, tiled=True
        ),
        lax.all_to_all(
            grad_aq.astype(jnp.bfloat16), "frame", split_axis=0, concat_axis=2, tiled=True
        ),
        lax.all_to_all(
            grad_ak.astype(jnp.bfloat16), "frame", split_axis=0, concat_axis=2, tiled=True
        ),
        lax.all_to_all(
            grad_av.astype(jnp.bfloat16), "frame", split_axis=0, concat_axis=2, tiled=True
        ),
    )
    return (returned[0], returned[1], returned[2], returned[3], returned[4], returned[5])


def solution(mesh):
    return jax.shard_map(
        shards,
        mesh=mesh,
        in_specs=(
            P("frame", "seq", None),
            P("frame", "seq", None),
            P("frame", "seq", None),
            P("frame", "seq", None),
            P("frame", "seq", None),
            P("frame", "seq", None),
            P("frame", "seq", None),
            P("frame", "seq", None),
            P(),
            P(),
        ),
        out_specs=(
            P("frame", "seq", None),
            P("frame", "seq", None),
            P("frame", "seq", None),
            P("frame", "seq", None),
            P("frame", "seq", None),
            P("frame", "seq", None),
        ),
        check_vma=False,
    )
```

profile of v0, /device:TPU:25, one launch (start us, length us, event | category | flops | bytes accessed | tf_op | source)
XLA Modules:
  0.0 365.3 jit_solution(8024674353530809530)
XLA Ops:
  3.3 11.5 %reduce.15 = bf16[2048,32]{1,0:T(8,128)(2,1)S(1)} reduce(bf16[2048,1,32]{2,1,0:T(2,128)(2,1)S(1)} %bitcast.217, bf16[]{:T(256)} %broadcast.141), dimensions={1}, to_apply=%bitcast.192.reduce_sub_computation | reduce | bytes 262146
  16.0 3.6 all-to-all-start
  20.3 11.5 %reduce.14 = bf16[2048,32]{1,0:T(8,128)(2,1)S(1)} reduce(bf16[2048,1,32]{2,1,0:T(2,128)(2,1)S(1)} %bitcast.223, bf16[]{:T(256)} %broadcast.141), dimensions={1}, to_apply=%bitcast.190.reduce_sub_computation | reduce | bytes 262146
  33.0 3.9 %all-to-all-start.1 = ((bf16[4,2,8192]{2,1,0:T(2,128)(2,1)}), bf16[4,2,8192]{2,1,0:T(2,128)(2,1)S(1)}, u32[]{:S(2)}, u32[]{:S(2)}) async-start(bf16[4,2,8192]{2,1,0:T(2,128)(2,1)} %reshape.238), calls=%async_computation.1 | async-start | bytes 262144 | tf_op jit(solution)/shard_map/all_to_all | solution.py:53
  37.7 11.5 %reduce.10 = bf16[2048,96]{1,0:T(8,128)(2,1)S(1)} reduce(bf16[2048,1,96]{2,1,0:T(2,128)(2,1)S(1)} %bitcast.224, bf16[]{:T(256)} %broadcast.141), dimensions={1}, to_apply=%bitcast.200.reduce_sub_computation | reduce | bytes 786434
  51.6 20.8 %reduce.13 = bf16[2048,96]{1,0:T(8,128)(2,1)S(1)} reduce(bf16[2048,1,96]{2,1,0:T(2,128)(2,1)S(1)} %bitcast.225, bf16[]{:T(256)} %broadcast.141), dimensions={1}, to_apply=%bitcast.188.reduce_sub_computation | reduce | bytes 786434
  73.9 3.6 all-to-all-start.7
  77.7 4.6 %all-to-all-done.7 = bf16[4,2,24576]{2,1,0:T(2,128)(2,1)S(1)} async-done(((bf16[4,2,24576]{2,1,0:T(2,128)(2,1)}), bf16[4,2,24576]{2,1,0:T(2,128)(2,1)S(1)}, u32[]{:S(2)}, u32[]{:S(2)}) %all-to-all-start.7) | async-done | bytes 393248 | tf_op jit(solution)/shard_map/all_to_all | solution.py:55
  82.3 3.5 all-to-all-start.2
  86.6 11.5 %reduce.11 = bf16[2048,96]{1,0:T(8,128)(2,1)S(1)} reduce(bf16[2048,1,96]{2,1,0:T(2,128)(2,1)S(1)} %bitcast.226, bf16[]{:T(256)} %broadcast.141), dimensions={1}, to_apply=%bitcast.186.reduce_sub_computation | reduce | bytes 786434
  100.4 11.9 %reduce.12 = bf16[2048,96]{1,0:T(8,128)(2,1)S(1)} reduce(bf16[2048,1,96]{2,1,0:T(2,128)(2,1)S(1)} %bitcast.227, bf16[]{:T(256)} %broadcast.141), dimensions={1}, to_apply=%bitcast.198.reduce_sub_computation | reduce | bytes 786434
  114.6 3.6 all-to-all-start.3
  122.8 3.5 all-to-all-start.8
  141.4 11.5 %reduce.17 = bf16[2048,32]{1,0:T(8,128)(2,1)S(1)} reduce(bf16[2048,1,32]{2,1,0:T(2,128)(2,1)S(1)} %bitcast.228, bf16[]{:T(256)} %broadcast.141), dimensions={1}, to_apply=%bitcast.196.reduce_sub_computation | reduce | bytes 262146
  154.1 3.7 %all-to-all-start.4 = ((bf16[4,2,8192]{2,1,0:T(2,128)(2,1)}), bf16[4,2,8192]{2,1,0:T(2,128)(2,1)S(1)}, u32[]{:S(2)}, u32[]{:S(2)}) async-start(bf16[4,2,8192]{2,1,0:T(2,128)(2,1)} %reshape.244), calls=%async_computation.4 | async-start | bytes 262144 | tf_op jit(solution)/shard_map/all_to_all | solution.py:51
  159.2 9.0 %collective-permute-start.2 = (bf16[2,4,128,512]{3,2,1,0:T(8,128)(2,1)}, bf16[2,4,128,512]{3,2,1,0:T(8,128)(2,1)}, u32[]{:S(2)}, u32[]{:S(2)}) collective-permute-start(bf16[2,4,128,512]{3,2,1,0:T(8,128)(2,1)} %maximum_maximum_fusion), channel_id=1, source_target_pairs={{1,0},{2,1},{3,2},{4,3},{5,4},{6,5},{7,6},{9,8},{10,9},{11,10},{12... | collective-permute-start | bytes 3145736 | tf_op jit(solution)/shard_map/ppermute | solution.py:16
  169.1 11.5 %reduce.16 = bf16[2048,32]{1,0:T(8,128)(2,1)S(1)} reduce(bf16[2048,1,32]{2,1,0:T(2,128)(2,1)S(1)} %bitcast.222, bf16[]{:T(256)} %broadcast.141), dimensions={1}, to_apply=%bitcast.194.reduce_sub_computation | reduce | bytes 262146
  181.8 4.3 %collective-permute-start.3 = (bf16[2,4,128,512]{3,2,1,0:T(8,128)(2,1)}, bf16[2,4,128,512]{3,2,1,0:T(8,128)(2,1)}, u32[]{:S(2)}, u32[]{:S(2)}) collective-permute-start(bf16[2,4,128,512]{3,2,1,0:T(8,128)(2,1)} %maximum_maximum_fusion), channel_id=1, source_target_pairs={{2,0},{3,1},{4,2},{5,3},{6,4},{7,5},{10,8},{11,9},{12,10},{13,11},... | collective-permute-start | bytes 3145736 | tf_op jit(solution)/shard_map/ppermute | solution.py:16
  186.1 4.1 %all-to-all-start.5 = ((bf16[4,2,8192]{2,1,0:T(2,128)(2,1)}), bf16[4,2,8192]{2,1,0:T(2,128)(2,1)S(1)}, u32[]{:S(2)}, u32[]{:S(2)}) async-start(bf16[4,2,8192]{2,1,0:T(2,128)(2,1)} %reshape.242), calls=%async_computation.5 | async-start | bytes 262144 | tf_op jit(solution)/shard_map/all_to_all | solution.py:54
  199.2 6.9 %collective-permute-done.3 = bf16[2,4,128,512]{3,2,1,0:T(8,128)(2,1)} collective-permute-done((bf16[2,4,128,512]{3,2,1,0:T(8,128)(2,1)}, bf16[2,4,128,512]{3,2,1,0:T(8,128)(2,1)}, u32[]{:S(2)}, u32[]{:S(2)}) %collective-permute-start.3) | collective-permute-done | bytes 1048608 | tf_op jit(solution)/shard_map/ppermute | solution.py:16
  228.3 4.4 %reshape_squeeze.12 = bf16[4,480,4,128]{3,2,1,0:T(4,128)(2,1)} reshape(bf16[1,4,480,512]{3,2,1,0:T(8,128)(2,1)} %get-tuple-element.18) | data formatting | bytes 3932160 | tf_op jit(solution)/shard_map/reshape;squeeze | solution.py:88
  239.4 4.6 %convert_bitcast_fusion = bf16[4,480,4,128]{3,1,2,0:T(8,128)(2,1)} fusion(bf16[4,32,4,128]{3,2,0,1:T(4,128)(2,1)} %reshape.226, f32[4,4,32]{2,1,0:T(4,128)S(1)} %get-tuple-element.38, f32[4,4,32,480]{3,2,1,0:T(8,128)} %copy-done.11), kind=kOutput, calls=%fused_computation.20 | convolution fusion | flops 64635872 | bytes 3082240 | tf_op jit(solution)/shard_map/fhqk,fhqd->fhkd/dot_general | solution.py:133
  247.3 3.8 %copy.189 = bf16[4,480,4,128]{3,2,1,0:T(4,128)(2,1)} copy(bf16[4,480,4,128]{3,1,2,0:T(8,128)(2,1)} %convert_bitcast_fusion) | data formatting | bytes 3932160 | tf_op jit(solution)/shard_map/convert_element_type | solution.py:154
  261.1 4.3 %convert_element_type.140 = bf16[1,4,480,512]{3,2,1,0:T(8,128)(2,1)} reshape(bf16[4,480,4,128]{3,2,1,0:T(4,128)(2,1)} %copy.188) | data formatting | bytes 3932160 | tf_op jit(solution)/shard_map/convert_element_type | solution.py:153
  268.8 5.5 %collective-permute-start.4 = (bf16[2,4,128,512]{3,2,1,0:T(8,128)(2,1)}, bf16[2,4,128,512]{3,2,1,0:T(8,128)(2,1)}, u32[]{:S(2)}, u32[]{:S(2)}) collective-permute-start(bf16[2,4,128,512]{3,2,1,0:T(8,128)(2,1)} %pad_maximum_fusion), channel_id=1, source_target_pairs={{2,0},{3,1},{4,2},{5,3},{6,4},{7,5},{10,8},{11,9},{12,10},{13,11},... | collective-permute-start | bytes 3145736 | tf_op jit(solution)/shard_map/ppermute | solution.py:16
  275.4 5.4 %collective-permute-start.5 = (bf16[2,4,128,512]{3,2,1,0:T(8,128)(2,1)}, bf16[2,4,128,512]{3,2,1,0:T(8,128)(2,1)}, u32[]{:S(2)}, u32[]{:S(2)}) collective-permute-start(bf16[2,4,128,512]{3,2,1,0:T(8,128)(2,1)} %pad_maximum_fusion.1), channel_id=1, source_target_pairs={{1,0},{2,1},{3,2},{4,3},{5,4},{6,5},{7,6},{9,8},{10,9},{11,10},{12... | collective-permute-start | bytes 3145736 | tf_op jit(solution)/shard_map/ppermute | solution.py:16
  287.5 3.9 %all-to-all-start.6 = ((bf16[4,32,512]{2,1,0:T(8,128)(2,1)}), bf16[4,32,512]{2,1,0:T(8,128)(2,1)S(1)}, u32[]{:S(2)}, u32[]{:S(2)}) async-start(bf16[4,32,512]{2,1,0:T(8,128)(2,1)} %bitcast.212), calls=%async_computation.6 | async-start | bytes 262144 | tf_op jit(solution)/shard_map/all_to_all | solution.py:178
  293.8 25.5 %collective-permute-done.7 = bf16[2,4,128,512]{3,2,1,0:T(8,128)(2,1)} collective-permute-done((bf16[2,4,128,512]{3,2,1,0:T(8,128)(2,1)}, bf16[2,4,128,512]{3,2,1,0:T(8,128)(2,1)}, u32[]{:S(2)}, u32[]{:S(2)}) %collective-permute-start.7) | collective-permute-done | bytes 1048608 | tf_op jit(solution)/shard_map/ppermute | solution.py:16
  322.9 3.9 %all-to-all-start.10 = ((bf16[4,32,512]{2,1,0:T(8,128)(2,1)}), bf16[4,32,512]{2,1,0:T(8,128)(2,1)S(1)}, u32[]{:S(2)}, u32[]{:S(2)}) async-start(bf16[4,32,512]{2,1,0:T(8,128)(2,1)} %get-tuple-element.29), calls=%async_computation.10 | async-start | bytes 262144 | tf_op jit(solution)/shard_map/all_to_all | solution.py:184
  337.9 7.7 %all_to_all.240 = bf16[4,96,512]{2,1,0:T(8,128)(2,1)S(1)} all-to-all(bf16[4,96,512]{2,1,0:T(8,128)(2,1)S(1)} %get-tuple-element.31), channel_id=1, replica_groups=mesh['frame'=4,'seq'=8] {'frame'}, dimensions={0} | all-to-all | bytes 786432 | tf_op jit(solution)/shard_map/all_to_all | solution.py:193
  345.5 8.7 %all_to_all.241 = bf16[4,96,512]{2,1,0:T(8,128)(2,1)S(1)} all-to-all(bf16[4,96,512]{2,1,0:T(8,128)(2,1)S(1)} %get-tuple-element.32), channel_id=1, replica_groups=mesh['frame'=4,'seq'=8] {'frame'}, dimensions={0} | all-to-all | bytes 786432 | tf_op jit(solution)/shard_map/all_to_all | solution.py:190
  354.2 3.6 all-to-all-start.11
  (213 shorter events, 126.1 us)
Async XLA Ops:
  0.6 117.5 %copy-start = (s32[4,8]{1,0:T(4,128)S(1)}, s32[4,8]{1,0:T(4,128)}, u32[]{:S(2)}) copy-start(s32[4,8]{1,0:T(4,128)} %param.22) | copy-start | bytes 388
  0.6 18.9 %copy-start.22 = (bf16[1,32,2048]{2,1,0:T(8,128)(2,1)S(1)}, bf16[1,32,2048]{2,1,0:T(8,128)(2,1)}, u32[]{:S(2)}) copy-start(bf16[1,32,2048]{2,1,0:T(8,128)(2,1)} %param.16) | copy-start | bytes 393220
  16.0 20.9 %copy-start.17 = (bf16[1,96,2048]{2,1,0:T(8,128)(2,1)S(1)}, bf16[1,96,2048]{2,1,0:T(8,128)(2,1)}, u32[]{:S(2)}) copy-start(bf16[1,96,2048]{2,1,0:T(8,128)(2,1)} %param.18) | copy-start | bytes 1179652
  16.0 17.0 %all-to-all-start = ((bf16[4,2,8192]{2,1,0:T(2,128)(2,1)}), bf16[4,2,8192]{2,1,0:T(2,128)(2,1)S(1)}, u32[]{:S(2)}, u32[]{:S(2)}) async-start(bf16[4,2,8192]{2,1,0:T(2,128)(2,1)} %reshape.240), calls=%async_computation | async-start | bytes 262144 | tf_op jit(solution)/shard_map/all_to_all | solution.py:52
  33.0 40.9 %all-to-all-start.1 = ((bf16[4,2,8192]{2,1,0:T(2,128)(2,1)}), bf16[4,2,8192]{2,1,0:T(2,128)(2,1)S(1)}, u32[]{:S(2)}, u32[]{:S(2)}) async-start(bf16[4,2,8192]{2,1,0:T(2,128)(2,1)} %reshape.238), calls=%async_computation.1 | async-start | bytes 262144 | tf_op jit(solution)/shard_map/all_to_all | solution.py:53
  36.9 13.9 %copy-start.18 = (bf16[1,96,2048]{2,1,0:T(8,128)(2,1)S(1)}, bf16[1,96,2048]{2,1,0:T(8,128)(2,1)}, u32[]{:S(2)}) copy-start(bf16[1,96,2048]{2,1,0:T(8,128)(2,1)} %param.19) | copy-start | bytes 1179652
  51.5 26.0 %copy-start.30 = (s32[4]{0:T(128)S(1)}, s32[4]{0:T(128)}, u32[]{:S(2)}) copy-start(s32[4]{0:T(128)} %param.23) | copy-start | bytes 52
  51.5 34.2 %copy-start.19 = (bf16[1,96,2048]{2,1,0:T(8,128)(2,1)S(1)}, bf16[1,96,2048]{2,1,0:T(8,128)(2,1)}, u32[]{:S(2)}) copy-start(bf16[1,96,2048]{2,1,0:T(8,128)(2,1)} %param.20) | copy-start | bytes 1179652
  73.9 8.4 %all-to-all-start.7 = ((bf16[4,2,24576]{2,1,0:T(2,128)(2,1)}), bf16[4,2,24576]{2,1,0:T(2,128)(2,1)S(1)}, u32[]{:S(2)}, u32[]{:S(2)}) async-start(bf16[4,2,24576]{2,1,0:T(2,128)(2,1)} %reshape.248), calls=%async_computation.7 | async-start | bytes 786432 | tf_op jit(solution)/shard_map/all_to_all | solution.py:55
  82.3 32.3 %all-to-all-start.2 = ((bf16[4,2,24576]{2,1,0:T(2,128)(2,1)}), bf16[4,2,24576]{2,1,0:T(2,128)(2,1)S(1)}, u32[]{:S(2)}, u32[]{:S(2)}) async-start(bf16[4,2,24576]{2,1,0:T(2,128)(2,1)} %reshape.236), calls=%async_computation.2 | async-start | bytes 786432 | tf_op jit(solution)/shard_map/all_to_all | solution.py:56
  85.8 13.9 %copy-start.20 = (bf16[1,96,2048]{2,1,0:T(8,128)(2,1)S(1)}, bf16[1,96,2048]{2,1,0:T(8,128)(2,1)}, u32[]{:S(2)}) copy-start(bf16[1,96,2048]{2,1,0:T(8,128)(2,1)} %param.21) | copy-start | bytes 1179652
  114.6 8.3 %all-to-all-start.3 = ((bf16[4,2,24576]{2,1,0:T(2,128)(2,1)}), bf16[4,2,24576]{2,1,0:T(2,128)(2,1)S(1)}, u32[]{:S(2)}, u32[]{:S(2)}) async-start(bf16[4,2,24576]{2,1,0:T(2,128)(2,1)} %reshape.234), calls=%async_computation.3 | async-start | bytes 786432 | tf_op jit(solution)/shard_map/all_to_all | solution.py:57
  122.8 12.5 %all-to-all-start.8 = ((bf16[4,2,24576]{2,1,0:T(2,128)(2,1)}), bf16[4,2,24576]{2,1,0:T(2,128)(2,1)S(1)}, u32[]{:S(2)}, u32[]{:S(2)}) async-start(bf16[4,2,24576]{2,1,0:T(2,128)(2,1)} %reshape.246), calls=%async_computation.8 | async-start | bytes 786432 | tf_op jit(solution)/shard_map/all_to_all | solution.py:58
  139.2 19.9 %copy-start.29 = (s32[4]{0:T(128)S(1)}, s32[4]{0:T(128)}, u32[]{:S(2)}) copy-start(s32[4]{0:T(128)} %get-tuple-element.12) | copy-start | bytes 52
  139.2 29.0 %copy-start.28 = (s32[4]{0:T(128)S(1)}, s32[4]{0:T(128)}, u32[]{:S(2)}) copy-start(s32[4]{0:T(128)} %get-tuple-element.11) | copy-start | bytes 52
  139.2 29.1 %copy-start.27 = (s32[4]{0:T(128)S(1)}, s32[4]{0:T(128)}, u32[]{:S(2)}) copy-start(s32[4]{0:T(128)} %get-tuple-element.8) | copy-start | bytes 52
  139.2 29.2 %copy-start.24 = (bf16[1,32,2048]{2,1,0:T(8,128)(2,1)S(1)}, bf16[1,32,2048]{2,1,0:T(8,128)(2,1)}, u32[]{:S(2)}) copy-start(bf16[1,32,2048]{2,1,0:T(8,128)(2,1)} %param.17) | copy-start | bytes 393220
  139.2 57.0 %collective-permute-start = (bf16[2,4,128,512]{3,2,1,0:T(8,128)(2,1)}, bf16[2,4,128,512]{3,2,1,0:T(8,128)(2,1)}, u32[]{:S(2)}, u32[]{:S(2)}) collective-permute-start(bf16[2,4,128,512]{3,2,1,0:T(8,128)(2,1)} %maximum_maximum_fusion), channel_id=1, source_target_pairs={{0,2},{1,3},{2,4},{3,5},{4,6},{5,7},{8,10},{9,11},{10,12},{11,13},... | collective-permute-start | bytes 3145736 | tf_op jit(solution)/shard_map/ppermute | solution.py:16
  154.1 36.1 %copy-start.26 = (s32[4]{0:T(128)S(1)}, s32[4]{0:T(128)}, u32[]{:S(2)}) copy-start(s32[4]{0:T(128)} %get-tuple-element.9) | copy-start | bytes 52
  154.1 32.0 %all-to-all-start.4 = ((bf16[4,2,8192]{2,1,0:T(2,128)(2,1)}), bf16[4,2,8192]{2,1,0:T(2,128)(2,1)S(1)}, u32[]{:S(2)}, u32[]{:S(2)}) async-start(bf16[4,2,8192]{2,1,0:T(2,128)(2,1)} %reshape.244), calls=%async_computation.4 | async-start | bytes 262144 | tf_op jit(solution)/shard_map/all_to_all | solution.py:51
  157.8 39.4 %collective-permute-start.1 = (bf16[2,4,128,512]{3,2,1,0:T(8,128)(2,1)}, bf16[2,4,128,512]{3,2,1,0:T(8,128)(2,1)}, u32[]{:S(2)}, u32[]{:S(2)}) collective-permute-start(bf16[2,4,128,512]{3,2,1,0:T(8,128)(2,1)} %maximum_maximum_fusion), channel_id=1, source_target_pairs={{0,1},{1,2},{2,3},{3,4},{4,5},{5,6},{6,7},{8,9},{9,10},{10,11},{11... | collective-permute-start | bytes 3145736 | tf_op jit(solution)/shard_map/ppermute | solution.py:16
  159.2 39.0 %collective-permute-start.2 = (bf16[2,4,128,512]{3,2,1,0:T(8,128)(2,1)}, bf16[2,4,128,512]{3,2,1,0:T(8,128)(2,1)}, u32[]{:S(2)}, u32[]{:S(2)}) collective-permute-start(bf16[2,4,128,512]{3,2,1,0:T(8,128)(2,1)} %maximum_maximum_fusion), channel_id=1, source_target_pairs={{1,0},{2,1},{3,2},{4,3},{5,4},{6,5},{7,6},{9,8},{10,9},{11,10},{12... | collective-permute-start | bytes 3145736 | tf_op jit(solution)/shard_map/ppermute | solution.py:16
  181.8 24.3 %collective-permute-start.3 = (bf16[2,4,128,512]{3,2,1,0:T(8,128)(2,1)}, bf16[2,4,128,512]{3,2,1,0:T(8,128)(2,1)}, u32[]{:S(2)}, u32[]{:S(2)}) collective-permute-start(bf16[2,4,128,512]{3,2,1,0:T(8,128)(2,1)} %maximum_maximum_fusion), channel_id=1, source_target_pairs={{2,0},{3,1},{4,2},{5,3},{6,4},{7,5},{10,8},{11,9},{12,10},{13,11},... | collective-permute-start | bytes 3145736 | tf_op jit(solution)/shard_map/ppermute | solution.py:16
  186.1 7.9 %all-to-all-start.5 = ((bf16[4,2,8192]{2,1,0:T(2,128)(2,1)}), bf16[4,2,8192]{2,1,0:T(2,128)(2,1)S(1)}, u32[]{:S(2)}, u32[]{:S(2)}) async-start(bf16[4,2,8192]{2,1,0:T(2,128)(2,1)} %reshape.242), calls=%async_computation.5 | async-start | bytes 262144 | tf_op jit(solution)/shard_map/all_to_all | solution.py:54
  268.8 25.0 %collective-permute-start.4 = (bf16[2,4,128,512]{3,2,1,0:T(8,128)(2,1)}, bf16[2,4,128,512]{3,2,1,0:T(8,128)(2,1)}, u32[]{:S(2)}, u32[]{:S(2)}) collective-permute-start(bf16[2,4,128,512]{3,2,1,0:T(8,128)(2,1)} %pad_maximum_fusion), channel_id=1, source_target_pairs={{2,0},{3,1},{4,2},{5,3},{6,4},{7,5},{10,8},{11,9},{12,10},{13,11},... | collective-permute-start | bytes 3145736 | tf_op jit(solution)/shard_map/ppermute | solution.py:16
  275.4 18.4 %collective-permute-start.5 = (bf16[2,4,128,512]{3,2,1,0:T(8,128)(2,1)}, bf16[2,4,128,512]{3,2,1,0:T(8,128)(2,1)}, u32[]{:S(2)}, u32[]{:S(2)}) collective-permute-start(bf16[2,4,128,512]{3,2,1,0:T(8,128)(2,1)} %pad_maximum_fusion.1), channel_id=1, source_target_pairs={{1,0},{2,1},{3,2},{4,3},{5,4},{6,5},{7,6},{9,8},{10,9},{11,10},{12... | collective-permute-start | bytes 3145736 | tf_op jit(solution)/shard_map/ppermute | solution.py:16
  282.0 11.8 %collective-permute-start.6 = (bf16[2,4,128,512]{3,2,1,0:T(8,128)(2,1)}, bf16[2,4,128,512]{3,2,1,0:T(8,128)(2,1)}, u32[]{:S(2)}, u32[]{:S(2)}) collective-permute-start(bf16[2,4,128,512]{3,2,1,0:T(8,128)(2,1)} %pad_maximum_fusion.2), channel_id=1, source_target_pairs={{0,1},{1,2},{2,3},{3,4},{4,5},{5,6},{6,7},{8,9},{9,10},{10,11},{11... | collective-permute-start | bytes 3145736 | tf_op jit(solution)/shard_map/ppermute | solution.py:16
  284.3 34.9 %collective-permute-start.7 = (bf16[2,4,128,512]{3,2,1,0:T(8,128)(2,1)}, bf16[2,4,128,512]{3,2,1,0:T(8,128)(2,1)}, u32[]{:S(2)}, u32[]{:S(2)}) collective-permute-start(bf16[2,4,128,512]{3,2,1,0:T(8,128)(2,1)} %pad_maximum_fusion.3), channel_id=1, source_target_pairs={{0,2},{1,3},{2,4},{3,5},{4,6},{5,7},{8,10},{9,11},{10,12},{11,13},... | collective-permute-start | bytes 3145736 | tf_op jit(solution)/shard_map/ppermute | solution.py:16
  287.5 35.4 %all-to-all-start.6 = ((bf16[4,32,512]{2,1,0:T(8,128)(2,1)}), bf16[4,32,512]{2,1,0:T(8,128)(2,1)S(1)}, u32[]{:S(2)}, u32[]{:S(2)}) async-start(bf16[4,32,512]{2,1,0:T(8,128)(2,1)} %bitcast.212), calls=%async_computation.6 | async-start | bytes 262144 | tf_op jit(solution)/shard_map/all_to_all | solution.py:178
  322.9 7.8 %all-to-all-start.10 = ((bf16[4,32,512]{2,1,0:T(8,128)(2,1)}), bf16[4,32,512]{2,1,0:T(8,128)(2,1)S(1)}, u32[]{:S(2)}, u32[]{:S(2)}) async-start(bf16[4,32,512]{2,1,0:T(8,128)(2,1)} %get-tuple-element.29), calls=%async_computation.10 | async-start | bytes 262144 | tf_op jit(solution)/shard_map/all_to_all | solution.py:184
  330.7 7.2 %all-to-all-start.9 = ((bf16[4,32,512]{2,1,0:T(8,128)(2,1)}), bf16[4,32,512]{2,1,0:T(8,128)(2,1)S(1)}, u32[]{:S(2)}, u32[]{:S(2)}) async-start(bf16[4,32,512]{2,1,0:T(8,128)(2,1)} %get-tuple-element.30), calls=%async_computation.9 | async-start | bytes 262144 | tf_op jit(solution)/shard_map/all_to_all | solution.py:181
  354.2 10.1 %all-to-all-start.11 = ((bf16[4,96,512]{2,1,0:T(8,128)(2,1)}), bf16[4,96,512]{2,1,0:T(8,128)(2,1)S(1)}, u32[]{:S(2)}, u32[]{:S(2)}) async-start(bf16[4,96,512]{2,1,0:T(8,128)(2,1)} %get-tuple-element.33), calls=%async_computation.11 | async-start | bytes 786432 | tf_op jit(solution)/shard_map/all_to_all | solution.py:187
  (20 other events, 87.2 us)
where the time goes:
time: 372 us; the launch traced here: 365 us
  other arithmetic  115 us (31%)
  local copies, waits for them, and re-layouts  84.4 us (23%)
  starting transfers between devices  73.7 us (20%)
  waiting for transfers between devices  52.4 us (14%)
  matrix products  21.6 us (6%)
  blocking collectives  16.3 us (4%)
    unnamed x10, other arithmetic  102 us
    unnamed x101, local copies, waits for them, and re-layouts  35.1 us
    ppermute x8, waiting for transfers between devices, from_behind(): return lax.ppermute(x, axis, pairs)  34.1 us
    ppermute x8, starting transfers between devices, from_behind(): return lax.ppermute(x, axis, pairs)  29.6 us
    all_to_all x1, blocking collectives, shards(): lax.all_to_all(grad_ak.astype(jnp.bfloat16), 'frame', split_axis=0, conca...  8.67 us
    all_to_all x1, blocking collectives, shards(): lax.all_to_all(grad_av.astype(jnp.bfloat16), 'frame', split_axis=0, conca...  7.66 us
  transfers between devices with their start and end apart: 20, of which 9 were waited for; matrix products, arithmetic and copies ran while one was open for 38% of the time, Pallas kernels for 0%

commit v1 on v0

v1 whole, which is shorter than its diff:
```python
import functools

import jax
import jax.numpy as jnp
from jax import lax
from jax.experimental import pallas as pl
from jax.experimental.pallas import tpu as pltpu
from jax.sharding import PartitionSpec as P

HD = 128
BAND = 2
SPAN = 2 * BAND + 1
NEG_BIG = -1e30


def from_behind(x, axis, by):
    peers = lax.axis_size(axis)
    pairs = [(i, i + by) for i in range(peers) if 0 <= i + by < peers]
    return lax.ppermute(x, axis, pairs)


def dot_nt(a, b):
    return lax.dot_general(a, b, (((1,), (1,)), ((), ())), preferred_element_type=jnp.float32)


def dot_tn(a, b):
    return lax.dot_general(a, b, (((0,), (0,)), ((), ())), preferred_element_type=jnp.float32)


def one_side(query, key_rows, val_rows, grad_out, mask):
    factor = HD ** (-0.5)
    scores = jnp.where(mask, dot_nt(query, key_rows) * factor, NEG_BIG)
    exponent = jnp.exp(scores - jnp.max(scores, axis=-1, keepdims=True))
    weights = exponent / jnp.sum(exponent, axis=-1, keepdims=True)
    half = weights.astype(jnp.bfloat16)
    output = jnp.dot(half, val_rows, preferred_element_type=jnp.float32)
    deltas = jnp.sum(grad_out.astype(jnp.float32) * output, axis=-1, keepdims=True)
    grad_weights = dot_nt(grad_out, val_rows)
    grad_scores = (weights * (grad_weights - deltas)).astype(jnp.bfloat16)
    grad_query = jnp.dot(grad_scores, key_rows, preferred_element_type=jnp.float32) * factor
    key_terms = dot_tn(grad_scores, query) * factor
    val_terms = dot_tn(half, grad_out)
    return tuple(x.astype(jnp.bfloat16) for x in (grad_query, key_terms, val_terms))


def block_kernel(heads, vr, ar, seq_count, match_ref, len_ref, here_ref, vq_ref, aq_ref, *refs):
    videos, audios = refs[:SPAN], refs[SPAN : 2 * SPAN]
    gvq_ref, gaq_ref = refs[2 * SPAN : 2 * SPAN + 2]
    video_terms = refs[2 * SPAN + 2 : 3 * SPAN + 2]
    audio_terms = refs[3 * SPAN + 2 :]
    group = match_ref[pl.program_id(0)]
    here = here_ref[0]
    slot = lax.broadcasted_iota(jnp.int32, (vr, SPAN * ar), 1)
    token = lax.broadcasted_iota(jnp.int32, (ar, SPAN * vr), 1)
    audio_live = slot < 0
    video_live = token < 0
    for p in range(SPAN):
        at = here + (p - BAND)
        inside = (at >= 0) & (at < seq_count)
        length = jnp.where(inside, len_ref[group, jnp.clip(at, 0, seq_count - 1)], 0)
        audio_live |= (slot >= p * ar) & (slot < p * ar + length)
        video_live |= (token >= p * vr) & (token < p * vr + jnp.where(inside, vr, 0))
    row = lax.broadcasted_iota(jnp.int32, (ar, HD), 0)
    own_live = row < len_ref[group, here]
    for h in range(heads):
        cols = slice(h * HD, (h + 1) * HD)
        grad, keys, vals = one_side(
            vq_ref[0, :vr, cols],
            jnp.concatenate([r[0, :ar, cols] for r in audios], axis=0),
            jnp.concatenate([r[0, ar:, cols] for r in audios], axis=0),
            vq_ref[0, vr:, cols],
            audio_live,
        )
        gvq_ref[0, :, cols] = grad
        for p in range(SPAN):
            audio_terms[p][0, :ar, cols] = keys[p * ar : (p + 1) * ar]
            audio_terms[p][0, ar:, cols] = vals[p * ar : (p + 1) * ar]
        audio_grad = aq_ref[0, ar:, cols]
        grad, keys, vals = one_side(
            aq_ref[0, :ar, cols],
            jnp.concatenate([r[0, :vr, cols] for r in videos], axis=0),
            jnp.concatenate([r[0, vr:, cols] for r in videos], axis=0),
            jnp.where(own_live, audio_grad, jnp.zeros_like(audio_grad)),
            video_live,
        )
        gaq_ref[0, :, cols] = grad
        for p in range(SPAN):
            video_terms[p][0, :vr, cols] = keys[p * vr : (p + 1) * vr]
            video_terms[p][0, vr:, cols] = vals[p * vr : (p + 1) * vr]


def spread(arrays, frames):
    rows = jnp.concatenate([a[0] for a in arrays], axis=0)
    width = rows.shape[1] // frames
    cut = jnp.stack([rows[:, i * width : (i + 1) * width] for i in range(frames)])
    return lax.all_to_all(cut, "frame", split_axis=0, concat_axis=0, tiled=True)


def shards(vid_q, vid_k, vid_v, vid_dout, aud_q, aud_k, aud_v, aud_dout, aud_len, match):
    frames = lax.axis_size("frame")
    seq_count = lax.axis_size("seq")
    here = lax.axis_index("seq").astype(jnp.int32).reshape(1)
    vr, ar = vid_q.shape[1], aud_q.shape[1]
    width = vid_q.shape[2] // frames
    offsets = range(-BAND, BAND + 1)
    sources = spread((aud_k, aud_v, vid_k, vid_v), frames)
    queries = spread((aud_q, aud_dout, vid_q, vid_dout), frames)
    nearby = [sources if o == 0 else from_behind(sources, "seq", -o) for o in offsets]

    tail = 2 * ar // (2 * vr)
    video_rows = pl.BlockSpec((1, 2 * vr, width), lambda f, m, l, w: (f, tail, 0))
    audio_rows = pl.BlockSpec((1, 2 * ar, width), lambda f, m, l, w: (m[f], 0, 0))
    video_own = pl.BlockSpec((1, 2 * vr, width), lambda f, m, l, w: (f, 0, 0))
    gvq_spec = pl.BlockSpec((1, vr, width), lambda f, m, l, w: (f, 0, 0))
    gaq_spec = pl.BlockSpec((1, ar, width), lambda f, m, l, w: (m[f], 0, 0))

    def like(rows):
        return jax.ShapeDtypeStruct((frames, rows, width), jnp.bfloat16)

    flops = 2 * 6 * frames * width * 2 * vr * SPAN * ar
    outs = pl.pallas_call(
        functools.partial(block_kernel, width // HD, vr, ar, seq_count),
        out_shape=[like(vr), like(ar)] + [like(2 * vr)] * SPAN + [like(2 * ar)] * SPAN,
        grid_spec=pltpu.PrefetchScalarGridSpec(
            num_scalar_prefetch=3,
            grid=(frames,),
            in_specs=[video_rows, audio_rows] + [video_rows] * SPAN + [audio_rows] * SPAN,
            out_specs=[gvq_spec, gaq_spec] + [video_own] * SPAN + [audio_rows] * SPAN,
        ),
        compiler_params=pltpu.CompilerParams(vmem_limit_bytes=48 * 2**20),
        cost_estimate=pl.CostEstimate(
            flops=flops, bytes_accessed=12 * 2**20, transcendentals=flops // (12 * HD)
        ),
    )(match, aud_len, here, queries, queries, *nearby, *nearby)
    grad_vq, grad_aq = outs[:2]
    video_terms, audio_terms = outs[2 : 2 + SPAN], outs[2 + SPAN :]

    def gathered(terms):
        total = terms[BAND].astype(jnp.float32)
        for position, offset in enumerate(offsets):
            if offset != 0:
                total = total + from_behind(terms[position], "seq", offset).astype(jnp.float32)
        return total.astype(jnp.bfloat16)

    packed = jnp.concatenate(
        [gathered(audio_terms), grad_aq, gathered(video_terms), grad_vq], axis=1
    )
    back = lax.all_to_all(packed, "frame", split_axis=0, concat_axis=0, tiled=True)

    def whole(start, rows):
        parts = [back[i, start : start + rows] for i in range(frames)]
        return jnp.concatenate(parts, axis=1)[None]

    base = 3 * ar
    return (
        whole(base + 2 * vr, vr),
        whole(base, vr),
        whole(base + vr, vr),
        whole(2 * ar, ar),
        whole(0, ar),
        whole(ar, ar),
    )


def solution(mesh):
    token = P("frame", "seq", None)
    return jax.shard_map(
        shards,
        mesh=mesh,
        in_specs=(token,) * 8 + (P(), P()),
        out_specs=(token,) * 6,
        check_vma=False,
    )
```

time: 372 us -> 157 us (0.42); the launches traced: 365 us -> 156 us
  other arithmetic: 115 us -> 7.62 us
  local copies, waits for them, and re-layouts: 84.4 us -> 0.32 us
  starting transfers between devices: 73.7 us -> 31.5 us
  Pallas kernels: 0 us -> 23.3 us
  waiting for transfers between devices: 52.4 us -> 74.6 us
  matrix products: 21.6 us -> 0 us
    unnamed x10 -> x0, other arithmetic: 102 us -> none
    all_to_all x12 -> x2, starting transfers between devices: 44.1 us -> 7.31 us  [spread(): return lax.all_to_all(cut, 'frame', split_axis=0, concat_axis=0, tiled=True)]
    unnamed x101 -> x18, local copies, waits for them, and re-layouts: 35.1 us -> 0.03 us
    pallas_call x0 -> x1, Pallas kernels: none -> 23.3 us  [shards(): pl.pallas_call(functools.partial(block_kernel, width // HD, vr, ar, seq_c...]
    convert_element_type x10 -> x0, local copies, waits for them, and re-layouts: 21.7 us -> none  [the longest x2 7.2 us: shards(): joined(audio_value_terms).astype(jnp.bfloat16)]
    dot_general x11 -> x0, matrix products: 19.9 us -> none  [the longest x1 4.63 us: shards(): jnp.einsum('fhqk,fhqd->fhkd', video_side[1], split(video_grad), preferred...]
    ppermute x8 -> x12, waiting for transfers between devices: 34.1 us -> 48.5 us  [from_behind(): return lax.ppermute(x, axis, pairs)]
    all_to_all x12 -> x2, waiting for transfers between devices: 18.3 us -> 26.1 us  [spread(): return lax.all_to_all(cut, 'frame', split_axis=0, concat_axis=0, tiled=True)]
  transfers between devices with their start and end apart: 20 -> 14, of which waited for: 9 -> 4; matrix products, arithmetic and copies ran while one was open for 38% -> 1% of each run, Pallas kernels for 0% -> 0%
where the time goes in v1:
time: 157 us; the launch traced here: 156 us
  waiting for transfers between devices  74.6 us (48%)
  starting transfers between devices  31.5 us (20%)
  Pallas kernels  23.3 us (15%)
  blocking collectives  17.9 us (11%)
  other arithmetic  7.62 us (5%)
    ppermute x12, waiting for transfers between devices, from_behind(): return lax.ppermute(x, axis, pairs)  48.5 us
    all_to_all x2, waiting for transfers between devices, spread(): return lax.all_to_all(cut, 'frame', split_axis=0, concat_axis=0, tiled=True)  26.1 us
    ppermute x12, starting transfers between devices, from_behind(): return lax.ppermute(x, axis, pairs)  24.2 us
    pallas_call x1, Pallas kernels, shards(): pl.pallas_call(functools.partial(block_kernel, width // HD, vr, ar, seq_c...  23.3 us
    all_to_all x1, blocking collectives, shards(): lax.all_to_all(packed, 'frame', split_axis=0, concat_axis=0, tiled=True)  17.9 us
    all_to_all x2, starting transfers between devices, spread(): return lax.all_to_all(cut, 'frame', split_axis=0, concat_axis=0, tiled=True)  7.31 us
  transfers between devices with their start and end apart: 14, of which 4 were waited for; matrix products, arithmetic and copies ran while one was open for 1% of the time, Pallas kernels for 0%

profile of v1, /device:TPU:25, one launch (start us, length us, event | category | flops | bytes accessed | tf_op | source)
XLA Modules:
  0.0 156.1 jit_solution(16496968203316551712)
XLA Ops:
  0.6 1.3 pad_maximum_fusion.3
  2.0 0.1 slice_bitcast_fusion.3
  2.1 1.1 pad_maximum_fusion.4
  3.2 3.7 %all-to-all-start.1 = ((bf16[4,256,512]{2,1,0:T(8,128)(2,1)}), bf16[4,256,512]{2,1,0:T(8,128)(2,1)S(1)}, u32[]{:S(2)}, u32[]{:S(2)}) async-start(bf16[4,256,512]{2,1,0:T(8,128)(2,1)} %pad_maximum_fusion.4), calls=%async_computation.1 | async-start | bytes 2097152 | tf_op jit(solution)/shard_map/all_to_all | solution.py:96
  6.9 0.1 pad_maximum_fusion.1
  7.0 12.9 %all-to-all-done.1.refs_2_.refs_7_ = bf16[4,256,512]{2,1,0:T(8,128)(2,1)S(1)} async-done(((bf16[4,256,512]{2,1,0:T(8,128)(2,1)}), bf16[4,256,512]{2,1,0:T(8,128)(2,1)S(1)}, u32[]{:S(2)}, u32[]{:S(2)}) %all-to-all-start.1) | async-done | bytes 1048608 | tf_op jit(solution)/shard_map/all_to_all | solution.py:96
  19.9 2.1 %collective-permute-start.3 = (bf16[4,256,512]{2,1,0:T(8,128)(2,1)S(1)}, bf16[4,256,512]{2,1,0:T(8,128)(2,1)S(1)}, u32[]{:S(2)}, u32[]{:S(2)}) collective-permute-start(bf16[4,256,512]{2,1,0:T(8,128)(2,1)S(1)} %all-to-all-done.1.refs_2_.refs_7_), channel_id=1, source_target_pairs={{2,0},{3,1},{4,2},{5,3},{6,4},{7,5},{10,8},{11,9},{12,10},{13,11},... | collective-permute-start | bytes 3145736 | tf_op jit(solution)/shard_map/ppermute | solution.py:19
  22.1 4.6 %collective-permute-start.2 = (bf16[4,256,512]{2,1,0:T(8,128)(2,1)S(1)}, bf16[4,256,512]{2,1,0:T(8,128)(2,1)}, u32[]{:S(2)}, u32[]{:S(2)}) collective-permute-start(bf16[4,256,512]{2,1,0:T(8,128)(2,1)S(1)} %all-to-all-done.1.refs_2_.refs_7_), channel_id=1, source_target_pairs={{1,0},{2,1},{3,2},{4,3},{5,4},{6,5},{7,6},{9,8},{10,9},{11,10},{12... | collective-permute-start | bytes 3145736 | tf_op jit(solution)/shard_map/ppermute | solution.py:19
  26.7 1.3 collective-permute-start.1
  28.0 1.3 collective-permute-start
  29.4 1.2 pad_maximum_fusion.2
  30.5 3.6 %all-to-all-start = ((bf16[4,256,512]{2,1,0:T(8,128)(2,1)}), bf16[4,256,512]{2,1,0:T(8,128)(2,1)S(1)}, u32[]{:S(2)}, u32[]{:S(2)}) async-start(bf16[4,256,512]{2,1,0:T(8,128)(2,1)} %pad_maximum_fusion.2), calls=%async_computation | async-start | bytes 2097152 | tf_op jit(solution)/shard_map/all_to_all | solution.py:96
  34.2 13.1 %all-to-all-done.vq_ref.aq_ref = bf16[4,256,512]{2,1,0:T(8,128)(2,1)S(1)} async-done(((bf16[4,256,512]{2,1,0:T(8,128)(2,1)}), bf16[4,256,512]{2,1,0:T(8,128)(2,1)S(1)}, u32[]{:S(2)}, u32[]{:S(2)}) %all-to-all-start) | async-done | bytes 1048608 | tf_op jit(solution)/shard_map/all_to_all | solution.py:96
  47.4 16.4 %collective-permute-done.refs_0_.refs_5_ = bf16[4,256,512]{2,1,0:T(8,128)(2,1)} collective-permute-done((bf16[4,256,512]{2,1,0:T(8,128)(2,1)S(1)}, bf16[4,256,512]{2,1,0:T(8,128)(2,1)}, u32[]{:S(2)}, u32[]{:S(2)}) %collective-permute-start) | collective-permute-done | bytes 1048608 | tf_op jit(solution)/shard_map/ppermute | solution.py:19
  63.8 23.3 %shard_map.145 = (bf16[4,32,512]{2,1,0:T(8,128)(2,1)S(1)}, bf16[4,96,512]{2,1,0:T(8,128)(2,1)S(1)}, bf16[4,64,512]{2,1,0:T(8,128)(2,1)S(1)}, bf16[4,64,512]{2,1,...) custom-call(s32[4]{0:T(128)S(1)} %copy-done.1, ...), custom_call_target="tpu_custom_call" | custom-call | flops 754974720 | bytes 12582912 | tf_op jit(solution)/shard_map/pallas_call | solution.py:121
  87.1 2.0 %collective-permute-start.8 = (bf16[4,64,512]{2,1,0:T(8,128)(2,1)S(1)}, bf16[4,64,512]{2,1,0:T(8,128)(2,1)S(1)}, u32[]{:S(2)}, u32[]{:S(2)}) collective-permute-start(bf16[4,64,512]{2,1,0:T(8,128)(2,1)S(1)} %get-tuple-element.25), channel_id=1, source_target_pairs={{2,0},{3,1},{4,2},{5,3},{6,4},{7,5},{10,8},{11,9},{12,10},{13,11},... | collective-permute-start | bytes 786440 | tf_op jit(solution)/shard_map/ppermute | solution.py:19
  89.1 1.3 collective-permute-start.9
  90.5 1.3 collective-permute-start.10
  91.8 5.0 %collective-permute-start.4 = (bf16[4,192,512]{2,1,0:T(8,128)(2,1)S(1)}, bf16[4,192,512]{2,1,0:T(8,128)(2,1)S(1)}, u32[]{:S(2)}, u32[]{:S(2)}) collective-permute-start(bf16[4,192,512]{2,1,0:T(8,128)(2,1)S(1)} %get-tuple-element.19), channel_id=1, source_target_pairs={{2,0},{3,1},{4,2},{5,3},{6,4},{7,5},{10,8},{11,9},{12,10},{13,11},... | collective-permute-start | bytes 2359304 | tf_op jit(solution)/shard_map/ppermute | solution.py:19
  96.8 1.3 collective-permute-start.5
  98.2 1.3 collective-permute-start.6
  99.5 1.3 collective-permute-start.7
  100.8 1.3 collective-permute-start.11
  102.1 32.1 %collective-permute-done.11 = bf16[4,64,512]{2,1,0:T(8,128)(2,1)S(1)} collective-permute-done((bf16[4,64,512]{2,1,0:T(8,128)(2,1)S(1)}, bf16[4,64,512]{2,1,0:T(8,128)(2,1)S(1)}, u32[]{:S(2)}, u32[]{:S(2)}) %collective-permute-start.11) | collective-permute-done | bytes 262176 | tf_op jit(solution)/shard_map/ppermute | solution.py:19
  134.2 0.2 add_convert_fusion.1
  134.4 0.5 add_convert_fusion
  134.9 0.1 pad_maximum_fusion
  135.0 17.9 %all_to_all.15 = bf16[4,384,512]{2,1,0:T(8,128)(2,1)S(1)} all-to-all(bf16[4,384,512]{2,1,0:T(8,128)(2,1)S(1)} %pad_maximum_fusion), channel_id=1, replica_groups=mesh['frame'=4,'seq'=8] {'frame'}, dimensions={0} | all-to-all | bytes 3145728 | tf_op jit(solution)/shard_map/all_to_all | solution.py:148
  153.0 0.8 maximum_bitcast_fusion.2
  153.8 0.7 maximum_bitcast_fusion.5
  154.4 0.7 maximum_bitcast_fusion.3
  155.2 1.0 maximum_bitcast_fusion
  (31 shorter events, 0.3 us)
Async XLA Ops:
  3.2 3.7 %copy-start.5 = (bf16[1,96,2048]{2,1,0:T(8,128)(2,1)S(1)}, bf16[1,96,2048]{2,1,0:T(8,128)(2,1)}, u32[]{:S(2)}) copy-start(bf16[1,96,2048]{2,1,0:T(8,128)(2,1)} %param.17) | copy-start | bytes 1179652
  3.2 3.7 %copy-start.6 = (bf16[1,96,2048]{2,1,0:T(8,128)(2,1)S(1)}, bf16[1,96,2048]{2,1,0:T(8,128)(2,1)}, u32[]{:S(2)}) copy-start(bf16[1,96,2048]{2,1,0:T(8,128)(2,1)} %param.14) | copy-start | bytes 1179652
  3.2 3.7 %copy-start.7 = (bf16[1,32,2048]{2,1,0:T(8,128)(2,1)S(1)}, bf16[1,32,2048]{2,1,0:T(8,128)(2,1)}, u32[]{:S(2)}) copy-start(bf16[1,32,2048]{2,1,0:T(8,128)(2,1)} %param.13) | copy-start | bytes 393220
  3.2 3.7 %copy-start.8 = (bf16[1,32,2048]{2,1,0:T(8,128)(2,1)S(1)}, bf16[1,32,2048]{2,1,0:T(8,128)(2,1)}, u32[]{:S(2)}) copy-start(bf16[1,32,2048]{2,1,0:T(8,128)(2,1)} %param.10) | copy-start | bytes 393220
  3.2 16.7 %all-to-all-start.1 = ((bf16[4,256,512]{2,1,0:T(8,128)(2,1)}), bf16[4,256,512]{2,1,0:T(8,128)(2,1)S(1)}, u32[]{:S(2)}, u32[]{:S(2)}) async-start(bf16[4,256,512]{2,1,0:T(8,128)(2,1)} %pad_maximum_fusion.4), calls=%async_computation.1 | async-start | bytes 2097152 | tf_op jit(solution)/shard_map/all_to_all | solution.py:96
  19.9 10.6 %copy-start.2 = (bf16[4,256,512]{2,1,0:T(8,128)(2,1)}, bf16[4,256,512]{2,1,0:T(8,128)(2,1)S(1)}, u32[]{:S(2)}) copy-start(bf16[4,256,512]{2,1,0:T(8,128)(2,1)S(1)} %all-to-all-done.1.refs_2_.refs_7_) | copy-start | bytes 3145732
  19.9 27.4 %collective-permute-start.3 = (bf16[4,256,512]{2,1,0:T(8,128)(2,1)S(1)}, bf16[4,256,512]{2,1,0:T(8,128)(2,1)S(1)}, u32[]{:S(2)}, u32[]{:S(2)}) collective-permute-start(bf16[4,256,512]{2,1,0:T(8,128)(2,1)S(1)} %all-to-all-done.1.refs_2_.refs_7_), channel_id=1, source_target_pairs={{2,0},{3,1},{4,2},{5,3},{6,4},{7,5},{10,8},{11,9},{12,10},{13,11},... | collective-permute-start | bytes 3145736 | tf_op jit(solution)/shard_map/ppermute | solution.py:19
  22.1 25.3 %collective-permute-start.2 = (bf16[4,256,512]{2,1,0:T(8,128)(2,1)S(1)}, bf16[4,256,512]{2,1,0:T(8,128)(2,1)}, u32[]{:S(2)}, u32[]{:S(2)}) collective-permute-start(bf16[4,256,512]{2,1,0:T(8,128)(2,1)S(1)} %all-to-all-done.1.refs_2_.refs_7_), channel_id=1, source_target_pairs={{1,0},{2,1},{3,2},{4,3},{5,4},{6,5},{7,6},{9,8},{10,9},{11,10},{12... | collective-permute-start | bytes 3145736 | tf_op jit(solution)/shard_map/ppermute | solution.py:19
  26.7 20.7 %collective-permute-start.1 = (bf16[4,256,512]{2,1,0:T(8,128)(2,1)S(1)}, bf16[4,256,512]{2,1,0:T(8,128)(2,1)}, u32[]{:S(2)}, u32[]{:S(2)}) collective-permute-start(bf16[4,256,512]{2,1,0:T(8,128)(2,1)S(1)} %all-to-all-done.1.refs_2_.refs_7_), channel_id=1, source_target_pairs={{0,1},{1,2},{2,3},{3,4},{4,5},{5,6},{6,7},{8,9},{9,10},{10,11},{11... | collective-permute-start | bytes 3145736 | tf_op jit(solution)/shard_map/ppermute | solution.py:19
  28.0 35.8 %collective-permute-start = (bf16[4,256,512]{2,1,0:T(8,128)(2,1)S(1)}, bf16[4,256,512]{2,1,0:T(8,128)(2,1)}, u32[]{:S(2)}, u32[]{:S(2)}) collective-permute-start(bf16[4,256,512]{2,1,0:T(8,128)(2,1)S(1)} %all-to-all-done.1.refs_2_.refs_7_), channel_id=1, source_target_pairs={{0,2},{1,3},{2,4},{3,5},{4,6},{5,7},{8,10},{9,11},{10,12},{11,13},... | collective-permute-start | bytes 3145736 | tf_op jit(solution)/shard_map/ppermute | solution.py:19
  30.5 33.2 %copy-start = (s32[4,8]{1,0:T(4,128)S(1)}, s32[4,8]{1,0:T(4,128)}, u32[]{:S(2)}) copy-start(s32[4,8]{1,0:T(4,128)} %len_ref.1) | copy-start | bytes 388
  30.5 33.2 %copy-start.1 = (s32[4]{0:T(128)S(1)}, s32[4]{0:T(128)}, u32[]{:S(2)}) copy-start(s32[4]{0:T(128)} %match_ref.1) | copy-start | bytes 52
  30.5 16.8 %all-to-all-start = ((bf16[4,256,512]{2,1,0:T(8,128)(2,1)}), bf16[4,256,512]{2,1,0:T(8,128)(2,1)S(1)}, u32[]{:S(2)}, u32[]{:S(2)}) async-start(bf16[4,256,512]{2,1,0:T(8,128)(2,1)} %pad_maximum_fusion.2), calls=%async_computation | async-start | bytes 2097152 | tf_op jit(solution)/shard_map/all_to_all | solution.py:96
  47.4 16.4 %copy-start.3 = (bf16[4,256,512]{2,1,0:T(8,128)(2,1)}, bf16[4,256,512]{2,1,0:T(8,128)(2,1)S(1)}, u32[]{:S(2)}) copy-start(bf16[4,256,512]{2,1,0:T(8,128)(2,1)S(1)} %all-to-all-done.vq_ref.aq_ref) | copy-start | bytes 3145732
  47.4 16.4 %copy-start.4 = (bf16[4,256,512]{2,1,0:T(8,128)(2,1)}, bf16[4,256,512]{2,1,0:T(8,128)(2,1)S(1)}, u32[]{:S(2)}) copy-start(bf16[4,256,512]{2,1,0:T(8,128)(2,1)S(1)} %collective-permute-done.3.refs_4_.refs_9_) | copy-start | bytes 3145732
  87.1 11.0 %collective-permute-start.8 = (bf16[4,64,512]{2,1,0:T(8,128)(2,1)S(1)}, bf16[4,64,512]{2,1,0:T(8,128)(2,1)S(1)}, u32[]{:S(2)}, u32[]{:S(2)}) collective-permute-start(bf16[4,64,512]{2,1,0:T(8,128)(2,1)S(1)} %get-tuple-element.25), channel_id=1, source_target_pairs={{2,0},{3,1},{4,2},{5,3},{6,4},{7,5},{10,8},{11,9},{12,10},{13,11},... | collective-permute-start | bytes 786440 | tf_op jit(solution)/shard_map/ppermute | solution.py:19
  89.1 10.3 %collective-permute-start.9 = (bf16[4,64,512]{2,1,0:T(8,128)(2,1)S(1)}, bf16[4,64,512]{2,1,0:T(8,128)(2,1)S(1)}, u32[]{:S(2)}, u32[]{:S(2)}) collective-permute-start(bf16[4,64,512]{2,1,0:T(8,128)(2,1)S(1)} %get-tuple-element.26), channel_id=1, source_target_pairs={{1,0},{2,1},{3,2},{4,3},{5,4},{6,5},{7,6},{9,8},{10,9},{11,10},{12... | collective-permute-start | bytes 786440 | tf_op jit(solution)/shard_map/ppermute | solution.py:19
  90.5 10.3 %collective-permute-start.10 = (bf16[4,64,512]{2,1,0:T(8,128)(2,1)S(1)}, bf16[4,64,512]{2,1,0:T(8,128)(2,1)S(1)}, u32[]{:S(2)}, u32[]{:S(2)}) collective-permute-start(bf16[4,64,512]{2,1,0:T(8,128)(2,1)S(1)} %get-tuple-element.27), channel_id=1, source_target_pairs={{0,1},{1,2},{2,3},{3,4},{4,5},{5,6},{6,7},{8,9},{9,10},{10,11},{11... | collective-permute-start | bytes 786440 | tf_op jit(solution)/shard_map/ppermute | solution.py:19
  91.8 42.6 %collective-permute-start.4 = (bf16[4,192,512]{2,1,0:T(8,128)(2,1)S(1)}, bf16[4,192,512]{2,1,0:T(8,128)(2,1)S(1)}, u32[]{:S(2)}, u32[]{:S(2)}) collective-permute-start(bf16[4,192,512]{2,1,0:T(8,128)(2,1)S(1)} %get-tuple-element.19), channel_id=1, source_target_pairs={{2,0},{3,1},{4,2},{5,3},{6,4},{7,5},{10,8},{11,9},{12,10},{13,11},... | collective-permute-start | bytes 2359304 | tf_op jit(solution)/shard_map/ppermute | solution.py:19
  96.8 37.6 %collective-permute-start.5 = (bf16[4,192,512]{2,1,0:T(8,128)(2,1)S(1)}, bf16[4,192,512]{2,1,0:T(8,128)(2,1)S(1)}, u32[]{:S(2)}, u32[]{:S(2)}) collective-permute-start(bf16[4,192,512]{2,1,0:T(8,128)(2,1)S(1)} %get-tuple-element.20), channel_id=1, source_target_pairs={{1,0},{2,1},{3,2},{4,3},{5,4},{6,5},{7,6},{9,8},{10,9},{11,10},{12... | collective-permute-start | bytes 2359304 | tf_op jit(solution)/shard_map/ppermute | solution.py:19
  98.2 36.2 %collective-permute-start.6 = (bf16[4,192,512]{2,1,0:T(8,128)(2,1)S(1)}, bf16[4,192,512]{2,1,0:T(8,128)(2,1)S(1)}, u32[]{:S(2)}, u32[]{:S(2)}) collective-permute-start(bf16[4,192,512]{2,1,0:T(8,128)(2,1)S(1)} %get-tuple-element.21), channel_id=1, source_target_pairs={{0,1},{1,2},{2,3},{3,4},{4,5},{5,6},{6,7},{8,9},{9,10},{10,11},{11... | collective-permute-start | bytes 2359304 | tf_op jit(solution)/shard_map/ppermute | solution.py:19
  99.5 34.9 %collective-permute-start.7 = (bf16[4,192,512]{2,1,0:T(8,128)(2,1)S(1)}, bf16[4,192,512]{2,1,0:T(8,128)(2,1)S(1)}, u32[]{:S(2)}, u32[]{:S(2)}) collective-permute-start(bf16[4,192,512]{2,1,0:T(8,128)(2,1)S(1)} %get-tuple-element.22), channel_id=1, source_target_pairs={{0,2},{1,3},{2,4},{3,5},{4,6},{5,7},{8,10},{9,11},{10,12},{11,13},... | collective-permute-start | bytes 2359304 | tf_op jit(solution)/shard_map/ppermute | solution.py:19
  100.8 33.4 %collective-permute-start.11 = (bf16[4,64,512]{2,1,0:T(8,128)(2,1)S(1)}, bf16[4,64,512]{2,1,0:T(8,128)(2,1)S(1)}, u32[]{:S(2)}, u32[]{:S(2)}) collective-permute-start(bf16[4,64,512]{2,1,0:T(8,128)(2,1)S(1)} %get-tuple-element.28), channel_id=1, source_target_pairs={{0,2},{1,3},{2,4},{3,5},{4,6},{5,7},{8,10},{9,11},{10,12},{11,13},... | collective-permute-start | bytes 786440 | tf_op jit(solution)/shard_map/ppermute | solution.py:19

commit v2 on v1

v2 whole, which is shorter than its diff:
```python
import functools

import jax
import jax.numpy as jnp
from jax import lax
from jax.experimental import pallas as pl
from jax.experimental.pallas import tpu as pltpu
from jax.sharding import PartitionSpec as P

HD = 128
BAND = 2
SPAN = 2 * BAND + 1
NEG_BIG = -1e30


def from_behind(x, axis, by):
    peers = lax.axis_size(axis)
    pairs = [(i, i + by) for i in range(peers) if 0 <= i + by < peers]
    return lax.ppermute(x, axis, pairs)


def dot_nt(a, b):
    return lax.dot_general(a, b, (((1,), (1,)), ((), ())), preferred_element_type=jnp.float32)


def dot_tn(a, b):
    return lax.dot_general(a, b, (((0,), (0,)), ((), ())), preferred_element_type=jnp.float32)


def one_side(query, key_rows, val_rows, grad_out, mask):
    factor = HD ** (-0.5)
    scores = jnp.where(mask, dot_nt(query, key_rows) * factor, NEG_BIG)
    exponent = jnp.exp(scores - jnp.max(scores, axis=-1, keepdims=True))
    weights = exponent / jnp.sum(exponent, axis=-1, keepdims=True)
    half = weights.astype(jnp.bfloat16)
    output = jnp.dot(half, val_rows, preferred_element_type=jnp.float32)
    deltas = jnp.sum(grad_out.astype(jnp.float32) * output, axis=-1, keepdims=True)
    grad_weights = dot_nt(grad_out, val_rows)
    grad_scores = (weights * (grad_weights - deltas)).astype(jnp.bfloat16)
    grad_query = jnp.dot(grad_scores, key_rows, preferred_element_type=jnp.float32) * factor
    key_terms = dot_tn(grad_scores, query) * factor
    val_terms = dot_tn(half, grad_out)
    return tuple(x.astype(jnp.bfloat16) for x in (grad_query, key_terms, val_terms))


def block_kernel(frames, heads, vr, ar, seq_count, match_ref, len_ref, here_ref, own_ref, *refs):
    near, back_ref, terms = refs[:SPAN], refs[SPAN], refs[SPAN + 1 :]
    here = here_ref[0]
    split = 2 * ar
    slot = lax.broadcasted_iota(jnp.int32, (vr, SPAN * ar), 1)
    token = lax.broadcasted_iota(jnp.int32, (ar, SPAN * vr), 1)
    row = lax.broadcasted_iota(jnp.int32, (ar, HD), 0)

    def pair(f, carry):
        group = match_ref[f]
        audio_live = slot < 0
        video_live = token < 0
        for p in range(SPAN):
            at = here + (p - BAND)
            inside = (at >= 0) & (at < seq_count)
            length = jnp.where(inside, len_ref[group, jnp.clip(at, 0, seq_count - 1)], 0)
            audio_live |= (slot >= p * ar) & (slot < p * ar + length)
            video_live |= (token >= p * vr) & (token < p * vr + jnp.where(inside, vr, 0))
        own_live = row < len_ref[group, here]
        for h in range(heads):
            cols = slice(h * HD, (h + 1) * HD)
            grad, keys, vals = one_side(
                own_ref[f, split : split + vr, cols],
                jnp.concatenate([r[group, :ar, cols] for r in near], axis=0),
                jnp.concatenate([r[group, ar:split, cols] for r in near], axis=0),
                own_ref[f, split + vr :, cols],
                audio_live,
            )
            back_ref[f, ar:, cols] = grad
            for p in range(SPAN):
                terms[p][group, :ar, cols] = keys[p * ar : (p + 1) * ar]
                terms[p][group, ar:split, cols] = vals[p * ar : (p + 1) * ar]
            audio_grad = own_ref[group, ar:split, cols]
            grad, keys, vals = one_side(
                own_ref[group, :ar, cols],
                jnp.concatenate([r[f, split : split + vr, cols] for r in near], axis=0),
                jnp.concatenate([r[f, split + vr :, cols] for r in near], axis=0),
                jnp.where(own_live, audio_grad, jnp.zeros_like(audio_grad)),
                video_live,
            )
            back_ref[group, :ar, cols] = grad
            for p in range(SPAN):
                terms[p][f, split : split + vr, cols] = keys[p * vr : (p + 1) * vr]
                terms[p][f, split + vr :, cols] = vals[p * vr : (p + 1) * vr]
        return carry

    lax.fori_loop(0, frames, pair, 0)


def spread(arrays, frames):
    rows = jnp.concatenate([a[0] for a in arrays], axis=0)
    width = rows.shape[1] // frames
    cut = jnp.stack([rows[:, i * width : (i + 1) * width] for i in range(frames)])
    return lax.all_to_all(cut, "frame", split_axis=0, concat_axis=0, tiled=True)


def shards(vid_q, vid_k, vid_v, vid_dout, aud_q, aud_k, aud_v, aud_dout, aud_len, match):
    frames = lax.axis_size("frame")
    seq_count = lax.axis_size("seq")
    here = lax.axis_index("seq").astype(jnp.int32).reshape(1)
    vr, ar = vid_q.shape[1], aud_q.shape[1]
    width = vid_q.shape[2] // frames
    offsets = range(-BAND, BAND + 1)
    sources = spread((aud_k, aud_v, vid_k, vid_v), frames)
    queries = spread((aud_q, aud_dout, vid_q, vid_dout), frames)
    nearby = [sources if o == 0 else from_behind(sources, "seq", -o) for o in offsets]

    def like(rows):
        return jax.ShapeDtypeStruct((frames, rows, width), jnp.bfloat16)

    flops = 2 * 6 * frames * width * 2 * vr * SPAN * ar
    scalars = [pl.BlockSpec(memory_space=pltpu.SMEM)] * 3
    outs = pl.pallas_call(
        functools.partial(block_kernel, frames, width // HD, vr, ar, seq_count),
        out_shape=[like(vr + ar)] + [like(2 * (vr + ar))] * SPAN,
        in_specs=scalars + [pl.BlockSpec(memory_space=pltpu.VMEM)] * (1 + SPAN),
        out_specs=[pl.BlockSpec(memory_space=pltpu.VMEM)] * (1 + SPAN),
        compiler_params=pltpu.CompilerParams(vmem_limit_bytes=48 * 2**20),
        cost_estimate=pl.CostEstimate(
            flops=flops, bytes_accessed=12 * 2**20, transcendentals=flops // (12 * HD)
        ),
    )(match, aud_len, here, queries, *nearby)
    grads, terms = outs[0], outs[1:]

    def gathered(terms):
        total = terms[BAND].astype(jnp.float32)
        for position, offset in enumerate(offsets):
            if offset != 0:
                total = total + from_behind(terms[position], "seq", offset).astype(jnp.float32)
        return total.astype(jnp.bfloat16)

    packed = jnp.concatenate([gathered(terms), grads], axis=1)
    back = lax.all_to_all(packed, "frame", split_axis=0, concat_axis=0, tiled=True)

    def whole(start, rows):
        parts = [back[i, start : start + rows] for i in range(frames)]
        return jnp.concatenate(parts, axis=1)[None]

    base = 2 * (ar + vr)
    return (
        whole(base + ar, vr),
        whole(2 * ar, vr),
        whole(2 * ar + vr, vr),
        whole(base, ar),
        whole(0, ar),
        whole(ar, ar),
    )


def solution(mesh):
    token = P("frame", "seq", None)
    return jax.shard_map(
        shards,
        mesh=mesh,
        in_specs=(token,) * 8 + (P(), P()),
        out_specs=(token,) * 6,
        check_vma=False,
    )
```

time: 157 us -> 150 us (0.955)
  starting transfers between devices: 31.5 us -> 22.7 us
  waiting for transfers between devices: 74.6 us -> 79.1 us
  blocking collectives: 17.9 us -> 14.7 us
    ppermute x12 -> x8, starting transfers between devices: 24.2 us -> 15.4 us  [from_behind(): return lax.ppermute(x, axis, pairs)]
    ppermute x12 -> x8, waiting for transfers between devices: 48.5 us -> 53 us  [from_behind(): return lax.ppermute(x, axis, pairs)]
    all_to_all x1, blocking collectives: 17.9 us -> 14.7 us  [shards(): lax.all_to_all(packed, 'frame', split_axis=0, concat_axis=0, tiled=True)]
  transfers between devices with their start and end apart: 14 -> 10, of which waited for: 4 -> 5; matrix products, arithmetic and copies ran while one was open for 1% -> 1% of each run, Pallas kernels for 0% -> 0%
where the time goes in v2:
time: 150 us; the launch traced here: 149 us
  waiting for transfers between devices  79.1 us (53%)
  Pallas kernels  23.7 us (16%)
  starting transfers between devices  22.7 us (15%)
  blocking collectives  14.7 us (10%)
  other arithmetic  7.67 us (5%)
    ppermute x8, waiting for transfers between devices, from_behind(): return lax.ppermute(x, axis, pairs)  53 us
    all_to_all x2, waiting for transfers between devices, spread(): return lax.all_to_all(cut, 'frame', split_axis=0, concat_axis=0, tiled=True)  26.1 us
    pallas_call x1, Pallas kernels, shards(): pl.pallas_call(functools.partial(block_kernel, frames, width // HD, vr, a...  23.7 us
    ppermute x8, starting transfers between devices, from_behind(): return lax.ppermute(x, axis, pairs)  15.4 us
    all_to_all x1, blocking collectives, shards(): lax.all_to_all(packed, 'frame', split_axis=0, concat_axis=0, tiled=True)  14.7 us
    all_to_all x2, starting transfers between devices, spread(): return lax.all_to_all(cut, 'frame', split_axis=0, concat_axis=0, tiled=True)  7.31 us
    broadcast_in_dim x4, other arithmetic, whole(): return jnp.concatenate(parts, axis=1)[None]  3.13 us
  transfers between devices with their start and end apart: 10, of which 5 were waited for; matrix products, arithmetic and copies ran while one was open for 1% of the time, Pallas kernels for 0%

profile of v2, /device:TPU:25, one launch (start us, length us, event | category | flops | bytes accessed | tf_op | source)
XLA Modules:
  0.0 149.0 jit_solution(6639813935874275111)
XLA Ops:
  0.6 1.3 pad_maximum_fusion.3
  2.0 0.1 slice_bitcast_fusion.3
  2.1 1.1 pad_maximum_fusion.4
  3.2 3.7 %all-to-all-start.1 = ((bf16[4,256,512]{2,1,0:T(8,128)(2,1)}), bf16[4,256,512]{2,1,0:T(8,128)(2,1)S(1)}, u32[]{:S(2)}, u32[]{:S(2)}) async-start(bf16[4,256,512]{2,1,0:T(8,128)(2,1)} %pad_maximum_fusion.4), calls=%async_computation.1 | async-start | bytes 2097152 | tf_op jit(solution)/shard_map/all_to_all | solution.py:99
  6.9 0.1 pad_maximum_fusion.1
  7.0 12.9 %all-to-all-done.1.refs_2_ = bf16[4,256,512]{2,1,0:T(8,128)(2,1)S(1)} async-done(((bf16[4,256,512]{2,1,0:T(8,128)(2,1)}), bf16[4,256,512]{2,1,0:T(8,128)(2,1)S(1)}, u32[]{:S(2)}, u32[]{:S(2)}) %all-to-all-start.1) | async-done | bytes 1048608 | tf_op jit(solution)/shard_map/all_to_all | solution.py:99
  19.9 2.1 %collective-permute-start.3 = (bf16[4,256,512]{2,1,0:T(8,128)(2,1)S(1)}, bf16[4,256,512]{2,1,0:T(8,128)(2,1)S(1)}, u32[]{:S(2)}, u32[]{:S(2)}) collective-permute-start(bf16[4,256,512]{2,1,0:T(8,128)(2,1)S(1)} %all-to-all-done.1.refs_2_), channel_id=1, source_target_pairs={{2,0},{3,1},{4,2},{5,3},{6,4},{7,5},{10,8},{11,9},{12,10},{13,11},... | collective-permute-start | bytes 3145736 | tf_op jit(solution)/shard_map/ppermute | solution.py:19
  22.1 4.6 %collective-permute-start.2 = (bf16[4,256,512]{2,1,0:T(8,128)(2,1)S(1)}, bf16[4,256,512]{2,1,0:T(8,128)(2,1)}, u32[]{:S(2)}, u32[]{:S(2)}) collective-permute-start(bf16[4,256,512]{2,1,0:T(8,128)(2,1)S(1)} %all-to-all-done.1.refs_2_), channel_id=1, source_target_pairs={{1,0},{2,1},{3,2},{4,3},{5,4},{6,5},{7,6},{9,8},{10,9},{11,10},{12... | collective-permute-start | bytes 3145736 | tf_op jit(solution)/shard_map/ppermute | solution.py:19
  26.7 1.3 collective-permute-start.1
  28.0 1.3 collective-permute-start
  29.3 0.1 slice_bitcast_fusion.7
  29.4 1.1 pad_maximum_fusion.2
  30.6 3.6 %all-to-all-start = ((bf16[4,256,512]{2,1,0:T(8,128)(2,1)}), bf16[4,256,512]{2,1,0:T(8,128)(2,1)S(1)}, u32[]{:S(2)}, u32[]{:S(2)}) async-start(bf16[4,256,512]{2,1,0:T(8,128)(2,1)} %pad_maximum_fusion.2), calls=%async_computation | async-start | bytes 2097152 | tf_op jit(solution)/shard_map/all_to_all | solution.py:99
  34.2 13.1 %all-to-all-done.own_ref = bf16[4,256,512]{2,1,0:T(8,128)(2,1)S(1)} async-done(((bf16[4,256,512]{2,1,0:T(8,128)(2,1)}), bf16[4,256,512]{2,1,0:T(8,128)(2,1)S(1)}, u32[]{:S(2)}, u32[]{:S(2)}) %all-to-all-start) | async-done | bytes 1048608 | tf_op jit(solution)/shard_map/all_to_all | solution.py:99
  47.4 0.0 collective-permute-done.3.refs_4_
  47.4 0.0 collective-permute-done.2.refs_3_
  47.4 16.4 %collective-permute-done.refs_0_ = bf16[4,256,512]{2,1,0:T(8,128)(2,1)} collective-permute-done((bf16[4,256,512]{2,1,0:T(8,128)(2,1)S(1)}, bf16[4,256,512]{2,1,0:T(8,128)(2,1)}, u32[]{:S(2)}, u32[]{:S(2)}) %collective-permute-start) | collective-permute-done | bytes 1048608 | tf_op jit(solution)/shard_map/ppermute | solution.py:19
  63.8 23.7 %shard_map.145 = (bf16[4,128,512]{2,1,0:T(8,128)(2,1)S(1)}, bf16[4,256,512]{2,1,0:T(8,128)(2,1)S(1)}, bf16[4,256,512]{2,1,0:T(8,128)(2,1)S(1)}, bf16[4,256,512]{...) custom-call(s32[4]{0:T(128)S(1)} %copy-done.1, s32[4,8]{1,0:T(4,128)S(1)} %copy-done, ...), custom_call_target="tpu_custom_call" | custom-call | flops 754974720 | bytes 12582912 | tf_op jit(solution)/shard_map/pallas_call | solution.py:118
  87.5 2.1 %collective-permute-start.4 = (bf16[4,256,512]{2,1,0:T(8,128)(2,1)S(1)}, bf16[4,256,512]{2,1,0:T(8,128)(2,1)S(1)}, u32[]{:S(2)}, u32[]{:S(2)}) collective-permute-start(bf16[4,256,512]{2,1,0:T(8,128)(2,1)S(1)} %get-tuple-element.13), channel_id=1, source_target_pairs={{2,0},{3,1},{4,2},{5,3},{6,4},{7,5},{10,8},{11,9},{12,10},{13,11},... | collective-permute-start | bytes 3145736 | tf_op jit(solution)/shard_map/ppermute | solution.py:19
  89.6 1.4 collective-permute-start.5
  91.0 1.3 collective-permute-start.6
  92.3 1.3 collective-permute-start.7
  93.6 19.0 %collective-permute-done.4 = bf16[4,256,512]{2,1,0:T(8,128)(2,1)S(1)} collective-permute-done((bf16[4,256,512]{2,1,0:T(8,128)(2,1)S(1)}, bf16[4,256,512]{2,1,0:T(8,128)(2,1)S(1)}, u32[]{:S(2)}, u32[]{:S(2)}) %collective-permute-start.4) | collective-permute-done | bytes 1048608 | tf_op jit(solution)/shard_map/ppermute | solution.py:19
  112.6 17.6 %collective-permute-done.7 = bf16[4,256,512]{2,1,0:T(8,128)(2,1)S(1)} collective-permute-done((bf16[4,256,512]{2,1,0:T(8,128)(2,1)S(1)}, bf16[4,256,512]{2,1,0:T(8,128)(2,1)S(1)}, u32[]{:S(2)}, u32[]{:S(2)}) %collective-permute-start.7) | collective-permute-done | bytes 1048608 | tf_op jit(solution)/shard_map/ppermute | solution.py:19
  130.2 0.7 add_convert_fusion
  130.9 0.1 pad_maximum_fusion
  131.0 14.7 %all_to_all.15 = bf16[4,384,512]{2,1,0:T(8,128)(2,1)S(1)} all-to-all(bf16[4,384,512]{2,1,0:T(8,128)(2,1)S(1)} %pad_maximum_fusion), channel_id=1, replica_groups=mesh['frame'=4,'seq'=8] {'frame'}, dimensions={0} | all-to-all | bytes 3145728 | tf_op jit(solution)/shard_map/all_to_all | solution.py:138
  145.8 0.1 slice_bitcast_fusion.11
  145.8 0.8 maximum_bitcast_fusion.2
  146.6 0.7 maximum_bitcast_fusion.5
  147.3 0.7 maximum_bitcast_fusion.3
  148.0 1.0 maximum_bitcast_fusion
  (22 shorter events, 0.1 us)
Async XLA Ops:
  3.2 3.7 %copy-start.5 = (bf16[1,96,2048]{2,1,0:T(8,128)(2,1)S(1)}, bf16[1,96,2048]{2,1,0:T(8,128)(2,1)}, u32[]{:S(2)}) copy-start(bf16[1,96,2048]{2,1,0:T(8,128)(2,1)} %param.17) | copy-start | bytes 1179652
  3.2 3.7 %copy-start.6 = (bf16[1,96,2048]{2,1,0:T(8,128)(2,1)S(1)}, bf16[1,96,2048]{2,1,0:T(8,128)(2,1)}, u32[]{:S(2)}) copy-start(bf16[1,96,2048]{2,1,0:T(8,128)(2,1)} %param.14) | copy-start | bytes 1179652
  3.2 3.7 %copy-start.7 = (bf16[1,32,2048]{2,1,0:T(8,128)(2,1)S(1)}, bf16[1,32,2048]{2,1,0:T(8,128)(2,1)}, u32[]{:S(2)}) copy-start(bf16[1,32,2048]{2,1,0:T(8,128)(2,1)} %param.13) | copy-start | bytes 393220
  3.2 3.7 %copy-start.8 = (bf16[1,32,2048]{2,1,0:T(8,128)(2,1)S(1)}, bf16[1,32,2048]{2,1,0:T(8,128)(2,1)}, u32[]{:S(2)}) copy-start(bf16[1,32,2048]{2,1,0:T(8,128)(2,1)} %param.10) | copy-start | bytes 393220
  3.2 16.7 %all-to-all-start.1 = ((bf16[4,256,512]{2,1,0:T(8,128)(2,1)}), bf16[4,256,512]{2,1,0:T(8,128)(2,1)S(1)}, u32[]{:S(2)}, u32[]{:S(2)}) async-start(bf16[4,256,512]{2,1,0:T(8,128)(2,1)} %pad_maximum_fusion.4), calls=%async_computation.1 | async-start | bytes 2097152 | tf_op jit(solution)/shard_map/all_to_all | solution.py:99
  19.9 10.6 %copy-start.2 = (bf16[4,256,512]{2,1,0:T(8,128)(2,1)}, bf16[4,256,512]{2,1,0:T(8,128)(2,1)S(1)}, u32[]{:S(2)}) copy-start(bf16[4,256,512]{2,1,0:T(8,128)(2,1)S(1)} %all-to-all-done.1.refs_2_) | copy-start | bytes 3145732
  19.9 27.4 %collective-permute-start.3 = (bf16[4,256,512]{2,1,0:T(8,128)(2,1)S(1)}, bf16[4,256,512]{2,1,0:T(8,128)(2,1)S(1)}, u32[]{:S(2)}, u32[]{:S(2)}) collective-permute-start(bf16[4,256,512]{2,1,0:T(8,128)(2,1)S(1)} %all-to-all-done.1.refs_2_), channel_id=1, source_target_pairs={{2,0},{3,1},{4,2},{5,3},{6,4},{7,5},{10,8},{11,9},{12,10},{13,11},... | collective-permute-start | bytes 3145736 | tf_op jit(solution)/shard_map/ppermute | solution.py:19
  22.1 25.3 %collective-permute-start.2 = (bf16[4,256,512]{2,1,0:T(8,128)(2,1)S(1)}, bf16[4,256,512]{2,1,0:T(8,128)(2,1)}, u32[]{:S(2)}, u32[]{:S(2)}) collective-permute-start(bf16[4,256,512]{2,1,0:T(8,128)(2,1)S(1)} %all-to-all-done.1.refs_2_), channel_id=1, source_target_pairs={{1,0},{2,1},{3,2},{4,3},{5,4},{6,5},{7,6},{9,8},{10,9},{11,10},{12... | collective-permute-start | bytes 3145736 | tf_op jit(solution)/shard_map/ppermute | solution.py:19
  26.7 20.7 %collective-permute-start.1 = (bf16[4,256,512]{2,1,0:T(8,128)(2,1)S(1)}, bf16[4,256,512]{2,1,0:T(8,128)(2,1)}, u32[]{:S(2)}, u32[]{:S(2)}) collective-permute-start(bf16[4,256,512]{2,1,0:T(8,128)(2,1)S(1)} %all-to-all-done.1.refs_2_), channel_id=1, source_target_pairs={{0,1},{1,2},{2,3},{3,4},{4,5},{5,6},{6,7},{8,9},{9,10},{10,11},{11... | collective-permute-start | bytes 3145736 | tf_op jit(solution)/shard_map/ppermute | solution.py:19
  28.0 35.8 %collective-permute-start = (bf16[4,256,512]{2,1,0:T(8,128)(2,1)S(1)}, bf16[4,256,512]{2,1,0:T(8,128)(2,1)}, u32[]{:S(2)}, u32[]{:S(2)}) collective-permute-start(bf16[4,256,512]{2,1,0:T(8,128)(2,1)S(1)} %all-to-all-done.1.refs_2_), channel_id=1, source_target_pairs={{0,2},{1,3},{2,4},{3,5},{4,6},{5,7},{8,10},{9,11},{10,12},{11,13},... | collective-permute-start | bytes 3145736 | tf_op jit(solution)/shard_map/ppermute | solution.py:19
  30.5 33.2 %copy-start = (s32[4,8]{1,0:T(4,128)S(1)}, s32[4,8]{1,0:T(4,128)}, u32[]{:S(2)}) copy-start(s32[4,8]{1,0:T(4,128)} %len_ref.1) | copy-start | bytes 388
  30.6 33.2 %copy-start.1 = (s32[4]{0:T(128)S(1)}, s32[4]{0:T(128)}, u32[]{:S(2)}) copy-start(s32[4]{0:T(128)} %match_ref.1) | copy-start | bytes 52
  30.6 16.8 %all-to-all-start = ((bf16[4,256,512]{2,1,0:T(8,128)(2,1)}), bf16[4,256,512]{2,1,0:T(8,128)(2,1)S(1)}, u32[]{:S(2)}, u32[]{:S(2)}) async-start(bf16[4,256,512]{2,1,0:T(8,128)(2,1)} %pad_maximum_fusion.2), calls=%async_computation | async-start | bytes 2097152 | tf_op jit(solution)/shard_map/all_to_all | solution.py:99
  47.4 16.4 %copy-start.3 = (bf16[4,256,512]{2,1,0:T(8,128)(2,1)}, bf16[4,256,512]{2,1,0:T(8,128)(2,1)S(1)}, u32[]{:S(2)}) copy-start(bf16[4,256,512]{2,1,0:T(8,128)(2,1)S(1)} %all-to-all-done.own_ref) | copy-start | bytes 3145732
  47.4 16.4 %copy-start.4 = (bf16[4,256,512]{2,1,0:T(8,128)(2,1)}, bf16[4,256,512]{2,1,0:T(8,128)(2,1)S(1)}, u32[]{:S(2)}) copy-start(bf16[4,256,512]{2,1,0:T(8,128)(2,1)S(1)} %collective-permute-done.3.refs_4_) | copy-start | bytes 3145732
  87.5 25.0 %collective-permute-start.4 = (bf16[4,256,512]{2,1,0:T(8,128)(2,1)S(1)}, bf16[4,256,512]{2,1,0:T(8,128)(2,1)S(1)}, u32[]{:S(2)}, u32[]{:S(2)}) collective-permute-start(bf16[4,256,512]{2,1,0:T(8,128)(2,1)S(1)} %get-tuple-element.13), channel_id=1, source_target_pairs={{2,0},{3,1},{4,2},{5,3},{6,4},{7,5},{10,8},{11,9},{12,10},{13,11},... | collective-permute-start | bytes 3145736 | tf_op jit(solution)/shard_map/ppermute | solution.py:19
  89.6 23.0 %collective-permute-start.5 = (bf16[4,256,512]{2,1,0:T(8,128)(2,1)S(1)}, bf16[4,256,512]{2,1,0:T(8,128)(2,1)S(1)}, u32[]{:S(2)}, u32[]{:S(2)}) collective-permute-start(bf16[4,256,512]{2,1,0:T(8,128)(2,1)S(1)} %get-tuple-element.14), channel_id=1, source_target_pairs={{1,0},{2,1},{3,2},{4,3},{5,4},{6,5},{7,6},{9,8},{10,9},{11,10},{12... | collective-permute-start | bytes 3145736 | tf_op jit(solution)/shard_map/ppermute | solution.py:19
  91.0 21.6 %collective-permute-start.6 = (bf16[4,256,512]{2,1,0:T(8,128)(2,1)S(1)}, bf16[4,256,512]{2,1,0:T(8,128)(2,1)S(1)}, u32[]{:S(2)}, u32[]{:S(2)}) collective-permute-start(bf16[4,256,512]{2,1,0:T(8,128)(2,1)S(1)} %get-tuple-element.15), channel_id=1, source_target_pairs={{0,1},{1,2},{2,3},{3,4},{4,5},{5,6},{6,7},{8,9},{9,10},{10,11},{11... | collective-permute-start | bytes 3145736 | tf_op jit(solution)/shard_map/ppermute | solution.py:19
  92.3 37.9 %collective-permute-start.7 = (bf16[4,256,512]{2,1,0:T(8,128)(2,1)S(1)}, bf16[4,256,512]{2,1,0:T(8,128)(2,1)S(1)}, u32[]{:S(2)}, u32[]{:S(2)}) collective-permute-start(bf16[4,256,512]{2,1,0:T(8,128)(2,1)S(1)} %get-tuple-element.16), channel_id=1, source_target_pairs={{0,2},{1,3},{2,4},{3,5},{4,6},{5,7},{8,10},{9,11},{10,12},{11,13},... | collective-permute-start | bytes 3145736 | tf_op jit(solution)/shard_map/ppermute | solution.py:19

commit v3 on v2

--- a/solution.py
+++ b/solution.py
@@ -17,6 +17,11 @@
     peers = lax.axis_size(axis)
     pairs = [(i, i + by) for i in range(peers) if 0 <= i + by < peers]
     return lax.ppermute(x, axis, pairs)
+
+
+def to_partner(x, axis):
+    peers = lax.axis_size(axis)
+    return lax.ppermute(x, axis, [(i, i ^ 1) for i in range(peers)])
 
 
 def dot_nt(a, b):
@@ -44,7 +49,9 @@
 
 
 def block_kernel(frames, heads, vr, ar, seq_count, match_ref, len_ref, here_ref, own_ref, *refs):
-    near, back_ref, terms = refs[:SPAN], refs[SPAN], refs[SPAN + 1 :]
+    near, back_ref = refs[:SPAN], refs[SPAN]
+    far_behind, sides, centre, far_ahead = refs[SPAN + 1 :]
+    terms = (far_behind, sides.at[0], centre, sides.at[1], far_ahead)
     here = here_ref[0]
     split = 2 * ar
     slot = lax.broadcasted_iota(jnp.int32, (vr, SPAN * ar), 1)
@@ -105,36 +112,41 @@
     here = lax.axis_index("seq").astype(jnp.int32).reshape(1)
     vr, ar = vid_q.shape[1], aud_q.shape[1]
     width = vid_q.shape[2] // frames
-    offsets = range(-BAND, BAND + 1)
     sources = spread((aud_k, aud_v, vid_k, vid_v), frames)
     queries = spread((aud_q, aud_dout, vid_q, vid_dout), frames)
+    even = lax.rem(lax.axis_index("seq"), 2) == 0
+    offsets = range(-BAND, BAND + 1)
     nearby = [sources if o == 0 else from_behind(sources, "seq", -o) for o in offsets]
 
     def like(rows):
         return jax.ShapeDtypeStruct((frames, rows, width), jnp.bfloat16)
 
+    term = like(2 * (vr + ar))
+    both = jax.ShapeDtypeStruct((2,) + term.shape, term.dtype)
     flops = 2 * 6 * frames * width * 2 * vr * SPAN * ar
     scalars = [pl.BlockSpec(memory_space=pltpu.SMEM)] * 3
     outs = pl.pallas_call(
         functools.partial(block_kernel, frames, width // HD, vr, ar, seq_count),
-        out_shape=[like(vr + ar)] + [like(2 * (vr + ar))] * SPAN,
+        out_shape=[like(vr + ar), term, both, term, term],
         in_specs=scalars + [pl.BlockSpec(memory_space=pltpu.VMEM)] * (1 + SPAN),
-        out_specs=[pl.BlockSpec(memory_space=pltpu.VMEM)] * (1 + SPAN),
+        out_specs=[pl.BlockSpec(memory_space=pltpu.VMEM)] * 5,
         compiler_params=pltpu.CompilerParams(vmem_limit_bytes=48 * 2**20),
         cost_estimate=pl.CostEstimate(
             flops=flops, bytes_accessed=12 * 2**20, transcendentals=flops // (12 * HD)
         ),
     )(match, aud_len, here, queries, *nearby)
-    grads, terms = outs[0], outs[1:]
+    grads, far_behind, sides, centre, far_ahead = outs
+    got = to_partner(sides, "seq")
 
-    def gathered(terms):
-        total = terms[BAND].astype(jnp.float32)
-        for position, offset in enumerate(offsets):
-            if offset != 0:
-                total = total + from_behind(terms[position], "seq", offset).astype(jnp.float32)
-        return total.astype(jnp.bfloat16)
+    def wide(x):
+        return x.astype(jnp.float32)
 
-    packed = jnp.concatenate([gathered(terms), grads], axis=1)
+    sent_ahead = wide(far_ahead) + jnp.where(even, wide(got[1]), 0.0)
+    sent_behind = wide(far_behind) + jnp.where(even, 0.0, wide(got[0]))
+    total = wide(centre) + wide(jnp.where(even, got[0], got[1]))
+    total = total + wide(from_behind(sent_ahead.astype(jnp.bfloat16), "seq", BAND))
+    total = total + wide(from_behind(sent_behind.astype(jnp.bfloat16), "seq", -BAND))
+    packed = jnp.concatenate([total.astype(jnp.bfloat16), grads], axis=1)
     back = lax.all_to_all(packed, "frame", split_axis=0, concat_axis=0, tiled=True)
 
     def whole(start, rows):

time: 150 us -> 159 us (1.060)
  the two profiles are of different devices: /device:TPU:25 before, /device:TPU:0 now
where the time goes in v3:
time: 159 us; the launch traced here: 158 us
  waiting for transfers between devices  76.2 us (48%)
  Pallas kernels  24.4 us (15%)
  starting transfers between devices  22 us (14%)
  blocking collectives  21.6 us (14%)
  other arithmetic  9.78 us (6%)
  local copies, waits for them, and re-layouts  3.41 us (2%)
    ppermute x6, waiting for transfers between devices, from_behind(): return lax.ppermute(x, axis, pairs)  44.2 us
    all_to_all x2, waiting for transfers between devices, spread(): return lax.all_to_all(cut, 'frame', split_axis=0, concat_axis=0, tiled=True)  27.6 us
    pallas_call x1, Pallas kernels, shards(): pl.pallas_call(functools.partial(block_kernel, frames, width // HD, vr, a...  24.4 us
    all_to_all x1, blocking collectives, shards(): lax.all_to_all(packed, 'frame', split_axis=0, concat_axis=0, tiled=True)  21.6 us
    ppermute x6, starting transfers between devices, from_behind(): return lax.ppermute(x, axis, pairs)  13.3 us
    all_to_all x2, starting transfers between devices, spread(): return lax.all_to_all(cut, 'frame', split_axis=0, concat_axis=0, tiled=True)  8.68 us
    ppermute x1, waiting for transfers between devices, to_partner(): return lax.ppermute(x, axis, [(i, i ^ 1) for i in range(peers)])  4.37 us
  transfers between devices with their start and end apart: 9, of which 6 were waited for; matrix products, arithmetic and copies ran while one was open for 1% of the time, Pallas kernels for 0%

profile of v3, /device:TPU:0, one launch (start us, length us, event | category | flops | bytes accessed | tf_op | source)
XLA Modules:
  0.0 158.1 jit_solution(16590347432008521253)
XLA Ops:
  0.6 1.3 pad_maximum_fusion.3
  2.0 0.1 slice_bitcast_fusion.3
  2.1 1.1 pad_maximum_fusion.4
  3.2 5.2 %all-to-all-start.1 = ((bf16[4,256,512]{2,1,0:T(8,128)(2,1)}), bf16[4,256,512]{2,1,0:T(8,128)(2,1)S(1)}, u32[]{:S(2)}, u32[]{:S(2)}) async-start(bf16[4,256,512]{2,1,0:T(8,128)(2,1)} %pad_maximum_fusion.4), calls=%async_computation.1 | async-start | bytes 2097152 | tf_op jit(solution)/shard_map/all_to_all | solution.py:106
  8.4 0.1 pad_maximum_fusion.1
  8.5 13.5 %all-to-all-done.1.refs_2_ = bf16[4,256,512]{2,1,0:T(8,128)(2,1)S(1)} async-done(((bf16[4,256,512]{2,1,0:T(8,128)(2,1)}), bf16[4,256,512]{2,1,0:T(8,128)(2,1)S(1)}, u32[]{:S(2)}, u32[]{:S(2)}) %all-to-all-start.1) | async-done | bytes 1048608 | tf_op jit(solution)/shard_map/all_to_all | solution.py:106
  22.0 3.6 %collective-permute-start = (bf16[4,256,512]{2,1,0:T(8,128)(2,1)S(1)}, bf16[4,256,512]{2,1,0:T(8,128)(2,1)S(1)}, u32[]{:S(2)}, u32[]{:S(2)}) collective-permute-start(bf16[4,256,512]{2,1,0:T(8,128)(2,1)S(1)} %all-to-all-done.1.refs_2_), channel_id=1, source_target_pairs={{0,2},{1,3},{2,4},{3,5},{4,6},{5,7},{8,10},{9,11},{10,12},{11,13},... | collective-permute-start | bytes 3145736 | tf_op jit(solution)/shard_map/ppermute | solution.py:19
  25.6 2.3 %collective-permute-start.1 = (bf16[4,256,512]{2,1,0:T(8,128)(2,1)S(1)}, bf16[4,256,512]{2,1,0:T(8,128)(2,1)}, u32[]{:S(2)}, u32[]{:S(2)}) collective-permute-start(bf16[4,256,512]{2,1,0:T(8,128)(2,1)S(1)} %all-to-all-done.1.refs_2_), channel_id=1, source_target_pairs={{0,1},{1,2},{2,3},{3,4},{4,5},{5,6},{6,7},{8,9},{9,10},{10,11},{11... | collective-permute-start | bytes 3145736 | tf_op jit(solution)/shard_map/ppermute | solution.py:19
  27.9 1.3 collective-permute-start.2
  29.2 1.3 collective-permute-start.3
  30.6 1.1 pad_maximum_fusion.2
  31.7 3.5 %all-to-all-start = ((bf16[4,256,512]{2,1,0:T(8,128)(2,1)}), bf16[4,256,512]{2,1,0:T(8,128)(2,1)S(1)}, u32[]{:S(2)}, u32[]{:S(2)}) async-start(bf16[4,256,512]{2,1,0:T(8,128)(2,1)} %pad_maximum_fusion.2), calls=%async_computation | async-start | bytes 2097152 | tf_op jit(solution)/shard_map/all_to_all | solution.py:106
  35.3 14.1 %all-to-all-done.own_ref = bf16[4,256,512]{2,1,0:T(8,128)(2,1)S(1)} async-done(((bf16[4,256,512]{2,1,0:T(8,128)(2,1)}), bf16[4,256,512]{2,1,0:T(8,128)(2,1)S(1)}, u32[]{:S(2)}, u32[]{:S(2)}) %all-to-all-start) | async-done | bytes 1048608 | tf_op jit(solution)/shard_map/all_to_all | solution.py:106
  49.4 18.7 %collective-permute-done.3.refs_4_ = bf16[4,256,512]{2,1,0:T(8,128)(2,1)} collective-permute-done((bf16[4,256,512]{2,1,0:T(8,128)(2,1)S(1)}, bf16[4,256,512]{2,1,0:T(8,128)(2,1)}, u32[]{:S(2)}, u32[]{:S(2)}) %collective-permute-start.3) | collective-permute-done | bytes 1048608 | tf_op jit(solution)/shard_map/ppermute | solution.py:19
  68.1 24.4 %shard_map.145 = (bf16[4,128,512]{2,1,0:T(8,128)(2,1)S(1)}, bf16[4,256,512]{2,1,0:T(8,128)(2,1)S(1)}, bf16[2,4,256,512]{3,2,1,0:T(8,128)(2,1)}, bf16[4,256,512]{2,1,0:T(8,128)(2,1)S(1)}, bf16[4,256,512]{2,1,0:T(8,128)(2,1)S(1)}) custom-call(s32[4]{0:T(128)S(1)} %copy-done.5, s32[4,8]{1,0:T(4,128)S(1)} %copy-done.4, s32[1]{0:T(128)} %bitcast.here_ref, ...), custom_call_target="tpu_custom_call" | custom-call | flops 754974720 | bytes 12582912 | tf_op jit(solution)/shard_map/pallas_call | solution.py:128
  92.5 1.0 copy-done
  93.4 1.0 copy-done.1
  94.4 0.8 copy-done.2
  95.2 4.4 %collective-permute-done.4 = bf16[2,4,256,512]{3,2,1,0:T(8,128)(2,1)S(1)} collective-permute-done((bf16[2,4,256,512]{3,2,1,0:T(8,128)(2,1)}, bf16[2,4,256,512]{3,2,1,0:T(8,128)(2,1)S(1)}, u32[]{:S(2)}, u32[]{:S(2)}) %collective-permute-start.4) | collective-permute-done | bytes 2097184 | tf_op jit(solution)/shard_map/ppermute | solution.py:24
  99.6 2.2 %fusion.4 = (bf16[4,256,512]{2,1,0:T(8,128)(2,1)S(1)}, bf16[4,256,512]{2,1,0:T(8,128)(2,1)S(1)}) fusion(bf16[4,256,512]{2,1,0:T(8,128)(2,1)} %copy-done.1, pred[]{:T(512)S(6)} %eq.3, bf16[2,4,256,512]{3,2,1,0:T(8,128)(2,1)S(1)} %collective-permute-done.4, bf16[4,256,512]{2,1,0:T(8,128)(2,1)} %copy-done), kind=kLoop, calls=%fused_computation.7 | loop fusion | flops 5242880 | bytes 6291457 | tf_op jit(solution)/shard_map/convert_element_type | solution.py:147
  101.7 3.5 %collective-permute-start.5 = (bf16[4,256,512]{2,1,0:T(8,128)(2,1)S(1)}, bf16[4,256,512]{2,1,0:T(8,128)(2,1)S(1)}, u32[]{:S(2)}, u32[]{:S(2)}) collective-permute-start(bf16[4,256,512]{2,1,0:T(8,128)(2,1)S(1)} %get-tuple-element.16), channel_id=1, source_target_pairs={{0,2},{1,3},{2,4},{3,5},{4,6},{5,7},{8,10},{9,11},{10,12},{11,13},... | collective-permute-start | bytes 3145736 | tf_op jit(solution)/shard_map/ppermute | solution.py:19
  105.3 1.3 collective-permute-start.6
  106.6 21.3 %collective-permute-done.5 = bf16[4,256,512]{2,1,0:T(8,128)(2,1)S(1)} collective-permute-done((bf16[4,256,512]{2,1,0:T(8,128)(2,1)S(1)}, bf16[4,256,512]{2,1,0:T(8,128)(2,1)S(1)}, u32[]{:S(2)}, u32[]{:S(2)}) %collective-permute-start.5) | collective-permute-done | bytes 1048608 | tf_op jit(solution)/shard_map/ppermute | solution.py:19
  127.9 4.2 %collective-permute-done.6 = bf16[4,256,512]{2,1,0:T(8,128)(2,1)S(1)} collective-permute-done((bf16[4,256,512]{2,1,0:T(8,128)(2,1)S(1)}, bf16[4,256,512]{2,1,0:T(8,128)(2,1)S(1)}, u32[]{:S(2)}, u32[]{:S(2)}) %collective-permute-start.6) | collective-permute-done | bytes 1048608 | tf_op jit(solution)/shard_map/ppermute | solution.py:19
  132.1 0.7 fusion.2
  132.8 0.3 copy-done.3
  133.2 0.1 pad_maximum_fusion
  133.3 21.6 %all_to_all.15 = bf16[4,384,512]{2,1,0:T(8,128)(2,1)S(1)} all-to-all(bf16[4,384,512]{2,1,0:T(8,128)(2,1)S(1)} %pad_maximum_fusion), channel_id=1, replica_groups=mesh['frame'=4,'seq'=8] {'frame'}, dimensions={0} | all-to-all | bytes 3145728 | tf_op jit(solution)/shard_map/all_to_all | solution.py:150
  155.0 0.8 maximum_bitcast_fusion.2
  155.8 0.7 maximum_bitcast_fusion.5
  156.5 1.0 maximum_bitcast_fusion
  157.4 0.7 maximum_bitcast_fusion.3
  (25 shorter events, 0.3 us)
Async XLA Ops:
  2.1 6.3 %copy-start.7 = (bf16[1,96,2048]{2,1,0:T(8,128)(2,1)S(1)}, bf16[1,96,2048]{2,1,0:T(8,128)(2,1)}, u32[]{:S(2)}) copy-start(bf16[1,96,2048]{2,1,0:T(8,128)(2,1)} %param.17) | copy-start | bytes 1179652
  2.1 6.3 %copy-start.8 = (bf16[1,96,2048]{2,1,0:T(8,128)(2,1)S(1)}, bf16[1,96,2048]{2,1,0:T(8,128)(2,1)}, u32[]{:S(2)}) copy-start(bf16[1,96,2048]{2,1,0:T(8,128)(2,1)} %param.14) | copy-start | bytes 1179652
  2.1 6.3 %copy-start.9 = (bf16[1,32,2048]{2,1,0:T(8,128)(2,1)S(1)}, bf16[1,32,2048]{2,1,0:T(8,128)(2,1)}, u32[]{:S(2)}) copy-start(bf16[1,32,2048]{2,1,0:T(8,128)(2,1)} %param.13) | copy-start | bytes 393220
  2.1 6.3 %copy-start.10 = (bf16[1,32,2048]{2,1,0:T(8,128)(2,1)S(1)}, bf16[1,32,2048]{2,1,0:T(8,128)(2,1)}, u32[]{:S(2)}) copy-start(bf16[1,32,2048]{2,1,0:T(8,128)(2,1)} %param.10) | copy-start | bytes 393220
  3.2 18.8 %all-to-all-start.1 = ((bf16[4,256,512]{2,1,0:T(8,128)(2,1)}), bf16[4,256,512]{2,1,0:T(8,128)(2,1)S(1)}, u32[]{:S(2)}, u32[]{:S(2)}) async-start(bf16[4,256,512]{2,1,0:T(8,128)(2,1)} %pad_maximum_fusion.4), calls=%async_computation.1 | async-start | bytes 2097152 | tf_op jit(solution)/shard_map/all_to_all | solution.py:106
  22.0 9.7 %copy-start.6 = (bf16[4,256,512]{2,1,0:T(8,128)(2,1)}, bf16[4,256,512]{2,1,0:T(8,128)(2,1)S(1)}, u32[]{:S(2)}) copy-start(bf16[4,256,512]{2,1,0:T(8,128)(2,1)S(1)} %all-to-all-done.1.refs_2_) | copy-start | bytes 3145732
  22.0 27.3 %collective-permute-start = (bf16[4,256,512]{2,1,0:T(8,128)(2,1)S(1)}, bf16[4,256,512]{2,1,0:T(8,128)(2,1)S(1)}, u32[]{:S(2)}, u32[]{:S(2)}) collective-permute-start(bf16[4,256,512]{2,1,0:T(8,128)(2,1)S(1)} %all-to-all-done.1.refs_2_), channel_id=1, source_target_pairs={{0,2},{1,3},{2,4},{3,5},{4,6},{5,7},{8,10},{9,11},{10,12},{11,13},... | collective-permute-start | bytes 3145736 | tf_op jit(solution)/shard_map/ppermute | solution.py:19
  25.6 23.7 %collective-permute-start.1 = (bf16[4,256,512]{2,1,0:T(8,128)(2,1)S(1)}, bf16[4,256,512]{2,1,0:T(8,128)(2,1)}, u32[]{:S(2)}, u32[]{:S(2)}) collective-permute-start(bf16[4,256,512]{2,1,0:T(8,128)(2,1)S(1)} %all-to-all-done.1.refs_2_), channel_id=1, source_target_pairs={{0,1},{1,2},{2,3},{3,4},{4,5},{5,6},{6,7},{8,9},{9,10},{10,11},{11... | collective-permute-start | bytes 3145736 | tf_op jit(solution)/shard_map/ppermute | solution.py:19
  27.9 21.5 %collective-permute-start.2 = (bf16[4,256,512]{2,1,0:T(8,128)(2,1)S(1)}, bf16[4,256,512]{2,1,0:T(8,128)(2,1)}, u32[]{:S(2)}, u32[]{:S(2)}) collective-permute-start(bf16[4,256,512]{2,1,0:T(8,128)(2,1)S(1)} %all-to-all-done.1.refs_2_), channel_id=1, source_target_pairs={{1,0},{2,1},{3,2},{4,3},{5,4},{6,5},{7,6},{9,8},{10,9},{11,10},{12... | collective-permute-start | bytes 3145736 | tf_op jit(solution)/shard_map/ppermute | solution.py:19
  29.2 38.8 %collective-permute-start.3 = (bf16[4,256,512]{2,1,0:T(8,128)(2,1)S(1)}, bf16[4,256,512]{2,1,0:T(8,128)(2,1)}, u32[]{:S(2)}, u32[]{:S(2)}) collective-permute-start(bf16[4,256,512]{2,1,0:T(8,128)(2,1)S(1)} %all-to-all-done.1.refs_2_), channel_id=1, source_target_pairs={{2,0},{3,1},{4,2},{5,3},{6,4},{7,5},{10,8},{11,9},{12,10},{13,11},... | collective-permute-start | bytes 3145736 | tf_op jit(solution)/shard_map/ppermute | solution.py:19
  30.6 37.5 %copy-start.4 = (s32[4,8]{1,0:T(4,128)S(1)}, s32[4,8]{1,0:T(4,128)}, u32[]{:S(2)}) copy-start(s32[4,8]{1,0:T(4,128)} %len_ref.1) | copy-start | bytes 388
  30.6 37.4 %copy-start.5 = (s32[4]{0:T(128)S(1)}, s32[4]{0:T(128)}, u32[]{:S(2)}) copy-start(s32[4]{0:T(128)} %match_ref.1) | copy-start | bytes 52
  31.7 17.6 %all-to-all-start = ((bf16[4,256,512]{2,1,0:T(8,128)(2,1)}), bf16[4,256,512]{2,1,0:T(8,128)(2,1)S(1)}, u32[]{:S(2)}, u32[]{:S(2)}) async-start(bf16[4,256,512]{2,1,0:T(8,128)(2,1)} %pad_maximum_fusion.2), calls=%async_computation | async-start | bytes 2097152 | tf_op jit(solution)/shard_map/all_to_all | solution.py:106
  92.5 1.0 copy-start
  93.4 1.0 copy-start.1
  94.4 0.8 copy-start.2
  95.2 4.4 %collective-permute-start.4 = (bf16[2,4,256,512]{3,2,1,0:T(8,128)(2,1)}, bf16[2,4,256,512]{3,2,1,0:T(8,128)(2,1)S(1)}, u32[]{:S(2)}, u32[]{:S(2)}) collective-permute-start(bf16[2,4,256,512]{3,2,1,0:T(8,128)(2,1)} %get-tuple-element.12), channel_id=1, source_target_pairs={{0,1},{1,0},{2,3},{3,2},{4,5},{5,4},{6,7},{7,6},{8,9},{9,8},{10,11... | collective-permute-start | bytes 6291464 | tf_op jit(solution)/shard_map/ppermute | solution.py:24
  101.7 26.2 %collective-permute-start.5 = (bf16[4,256,512]{2,1,0:T(8,128)(2,1)S(1)}, bf16[4,256,512]{2,1,0:T(8,128)(2,1)S(1)}, u32[]{:S(2)}, u32[]{:S(2)}) collective-permute-start(bf16[4,256,512]{2,1,0:T(8,128)(2,1)S(1)} %get-tuple-element.16), channel_id=1, source_target_pairs={{0,2},{1,3},{2,4},{3,5},{4,6},{5,7},{8,10},{9,11},{10,12},{11,13},... | collective-permute-start | bytes 3145736 | tf_op jit(solution)/shard_map/ppermute | solution.py:19
  105.3 26.8 %collective-permute-start.6 = (bf16[4,256,512]{2,1,0:T(8,128)(2,1)S(1)}, bf16[4,256,512]{2,1,0:T(8,128)(2,1)S(1)}, u32[]{:S(2)}, u32[]{:S(2)}) collective-permute-start(bf16[4,256,512]{2,1,0:T(8,128)(2,1)S(1)} %get-tuple-element.17), channel_id=1, source_target_pairs={{2,0},{3,1},{4,2},{5,3},{6,4},{7,5},{10,8},{11,9},{12,10},{13,11},... | collective-permute-start | bytes 3145736 | tf_op jit(solution)/shard_map/ppermute | solution.py:19
  132.1 1.0 copy-start.3

commit v4 on v3

--- a/solution.py
+++ b/solution.py
@@ -49,9 +49,7 @@
 
 
 def block_kernel(frames, heads, vr, ar, seq_count, match_ref, len_ref, here_ref, own_ref, *refs):
-    near, back_ref = refs[:SPAN], refs[SPAN]
-    far_behind, sides, centre, far_ahead = refs[SPAN + 1 :]
-    terms = (far_behind, sides.at[0], centre, sides.at[1], far_ahead)
+    near, back_ref, terms = refs[:SPAN][::-1], refs[SPAN], refs[SPAN + 1 :]
     here = here_ref[0]
     split = 2 * ar
     slot = lax.broadcasted_iota(jnp.int32, (vr, SPAN * ar), 1)
@@ -116,27 +114,25 @@
     queries = spread((aud_q, aud_dout, vid_q, vid_dout), frames)
     even = lax.rem(lax.axis_index("seq"), 2) == 0
     offsets = range(-BAND, BAND + 1)
-    nearby = [sources if o == 0 else from_behind(sources, "seq", -o) for o in offsets]
+    nearby = [sources if o == 0 else from_behind(sources, "seq", -o) for o in reversed(offsets)]
 
     def like(rows):
         return jax.ShapeDtypeStruct((frames, rows, width), jnp.bfloat16)
 
-    term = like(2 * (vr + ar))
-    both = jax.ShapeDtypeStruct((2,) + term.shape, term.dtype)
     flops = 2 * 6 * frames * width * 2 * vr * SPAN * ar
     scalars = [pl.BlockSpec(memory_space=pltpu.SMEM)] * 3
     outs = pl.pallas_call(
         functools.partial(block_kernel, frames, width // HD, vr, ar, seq_count),
-        out_shape=[like(vr + ar), term, both, term, term],
+        out_shape=[like(vr + ar)] + [like(2 * (vr + ar))] * SPAN,
         in_specs=scalars + [pl.BlockSpec(memory_space=pltpu.VMEM)] * (1 + SPAN),
-        out_specs=[pl.BlockSpec(memory_space=pltpu.VMEM)] * 5,
+        out_specs=[pl.BlockSpec(memory_space=pltpu.VMEM)] * (1 + SPAN),
         compiler_params=pltpu.CompilerParams(vmem_limit_bytes=48 * 2**20),
         cost_estimate=pl.CostEstimate(
             flops=flops, bytes_accessed=12 * 2**20, transcendentals=flops // (12 * HD)
         ),
     )(match, aud_len, here, queries, *nearby)
-    grads, far_behind, sides, centre, far_ahead = outs
-    got = to_partner(sides, "seq")
+    grads, far_behind, near_behind, centre, near_ahead, far_ahead = outs
+    got = (to_partner(near_behind, "seq"), to_partner(near_ahead, "seq"))
 
     def wide(x):
         return x.astype(jnp.float32)

time: 159 us -> 155 us (0.975)
  waiting for transfers between devices: 76.2 us -> 59.6 us
  starting transfers between devices: 22 us -> 34 us
  local copies, waits for them, and re-layouts: 3.41 us -> 1.13 us
  other arithmetic: 9.78 us -> 12 us
    ppermute x6, waiting for transfers between devices: 44.2 us -> 28.4 us  [from_behind(): return lax.ppermute(x, axis, pairs)]
    ppermute x1 -> x2, starting transfers between devices: 0.01 us -> 8.3 us  [to_partner(): return lax.ppermute(x, axis, [(i, i ^ 1) for i in range(peers)])]
    ppermute x6, starting transfers between devices: 13.3 us -> 16.7 us  [from_behind(): return lax.ppermute(x, axis, pairs)]
    unnamed x22, local copies, waits for them, and re-layouts: 3.13 us -> 0.85 us
    ppermute x1 -> x2, waiting for transfers between devices: 4.37 us -> 2.63 us  [to_partner(): return lax.ppermute(x, axis, [(i, i ^ 1) for i in range(peers)])]
  transfers between devices with their start and end apart: 9 -> 10, of which waited for: 6 -> 6; matrix products, arithmetic and copies ran while one was open for 1% -> 3% of each run, Pallas kernels for 0% -> 0%
where the time goes in v4:
time: 155 us; the launch traced here: 154 us
  waiting for transfers between devices  59.6 us (38%)
  starting transfers between devices  34 us (22%)
  Pallas kernels  25 us (16%)
  blocking collectives  21.9 us (14%)
  other arithmetic  12 us (8%)
    all_to_all x2, waiting for transfers between devices, spread(): return lax.all_to_all(cut, 'frame', split_axis=0, concat_axis=0, tiled=True)  28.5 us
    ppermute x6, waiting for transfers between devices, from_behind(): return lax.ppermute(x, axis, pairs)  28.4 us
    pallas_call x1, Pallas kernels, shards(): pl.pallas_call(functools.partial(block_kernel, frames, width // HD, vr, a...  25 us
    all_to_all x1, blocking collectives, shards(): lax.all_to_all(packed, 'frame', split_axis=0, concat_axis=0, tiled=True)  21.9 us
    ppermute x6, starting transfers between devices, from_behind(): return lax.ppermute(x, axis, pairs)  16.7 us
    all_to_all x2, starting transfers between devices, spread(): return lax.all_to_all(cut, 'frame', split_axis=0, concat_axis=0, tiled=True)  8.95 us
    ppermute x2, starting transfers between devices, to_partner(): return lax.ppermute(x, axis, [(i, i ^ 1) for i in range(peers)])  8.3 us
    broadcast_in_dim x4, other arithmetic, whole(): return jnp.concatenate(parts, axis=1)[None]  3.13 us
  transfers between devices with their start and end apart: 10, of which 6 were waited for; matrix products, arithmetic and copies ran while one was open for 3% of the time, Pallas kernels for 0%

profile of v4, /device:TPU:0, one launch (start us, length us, event | category | flops | bytes accessed | tf_op | source)
XLA Modules:
  0.0 154.4 jit_solution(5894274727001577197)
XLA Ops:
  0.6 1.3 pad_maximum_fusion.3
  2.0 0.1 slice_bitcast_fusion.3
  2.1 1.1 pad_maximum_fusion.4
  3.2 5.3 %all-to-all-start.1 = ((bf16[4,256,512]{2,1,0:T(8,128)(2,1)}), bf16[4,256,512]{2,1,0:T(8,128)(2,1)S(1)}, u32[]{:S(2)}, u32[]{:S(2)}) async-start(bf16[4,256,512]{2,1,0:T(8,128)(2,1)} %pad_maximum_fusion.4), calls=%async_computation.1 | async-start | bytes 2097152 | tf_op jit(solution)/shard_map/all_to_all | solution.py:104
  8.5 0.1 pad_maximum_fusion.1
  8.6 13.5 %all-to-all-done.1.refs_2_ = bf16[4,256,512]{2,1,0:T(8,128)(2,1)S(1)} async-done(((bf16[4,256,512]{2,1,0:T(8,128)(2,1)}), bf16[4,256,512]{2,1,0:T(8,128)(2,1)S(1)}, u32[]{:S(2)}, u32[]{:S(2)}) %all-to-all-start.1) | async-done | bytes 1048608 | tf_op jit(solution)/shard_map/all_to_all | solution.py:104
  22.1 1.3 collective-permute-start
  23.4 1.3 collective-permute-start.1
  24.7 4.0 %collective-permute-start.2 = (bf16[4,256,512]{2,1,0:T(8,128)(2,1)S(1)}, bf16[4,256,512]{2,1,0:T(8,128)(2,1)}, u32[]{:S(2)}, u32[]{:S(2)}) collective-permute-start(bf16[4,256,512]{2,1,0:T(8,128)(2,1)S(1)} %all-to-all-done.1.refs_2_), channel_id=1, source_target_pairs={{0,1},{1,2},{2,3},{3,4},{4,5},{5,6},{6,7},{8,9},{9,10},{10,11},{11... | collective-permute-start | bytes 3145736 | tf_op jit(solution)/shard_map/ppermute | solution.py:19
  28.8 4.5 %collective-permute-start.3 = (bf16[4,256,512]{2,1,0:T(8,128)(2,1)S(1)}, bf16[4,256,512]{2,1,0:T(8,128)(2,1)}, u32[]{:S(2)}, u32[]{:S(2)}) collective-permute-start(bf16[4,256,512]{2,1,0:T(8,128)(2,1)S(1)} %all-to-all-done.1.refs_2_), channel_id=1, source_target_pairs={{0,2},{1,3},{2,4},{3,5},{4,6},{5,7},{8,10},{9,11},{10,12},{11,13},... | collective-permute-start | bytes 3145736 | tf_op jit(solution)/shard_map/ppermute | solution.py:19
  33.3 0.1 slice_bitcast_fusion.7
  33.4 1.1 pad_maximum_fusion.2
  34.5 3.6 %all-to-all-start = ((bf16[4,256,512]{2,1,0:T(8,128)(2,1)}), bf16[4,256,512]{2,1,0:T(8,128)(2,1)S(1)}, u32[]{:S(2)}, u32[]{:S(2)}) async-start(bf16[4,256,512]{2,1,0:T(8,128)(2,1)} %pad_maximum_fusion.2), calls=%async_computation | async-start | bytes 2097152 | tf_op jit(solution)/shard_map/all_to_all | solution.py:104
  38.2 15.0 %all-to-all-done.own_ref = bf16[4,256,512]{2,1,0:T(8,128)(2,1)S(1)} async-done(((bf16[4,256,512]{2,1,0:T(8,128)(2,1)}), bf16[4,256,512]{2,1,0:T(8,128)(2,1)S(1)}, u32[]{:S(2)}, u32[]{:S(2)}) %all-to-all-start) | async-done | bytes 1048608 | tf_op jit(solution)/shard_map/all_to_all | solution.py:104
  53.2 2.7 %collective-permute-done.3.refs_4_ = bf16[4,256,512]{2,1,0:T(8,128)(2,1)} collective-permute-done((bf16[4,256,512]{2,1,0:T(8,128)(2,1)S(1)}, bf16[4,256,512]{2,1,0:T(8,128)(2,1)}, u32[]{:S(2)}, u32[]{:S(2)}) %collective-permute-start.3) | collective-permute-done | bytes 1048608 | tf_op jit(solution)/shard_map/ppermute | solution.py:19
  55.9 25.0 %shard_map.145 = (bf16[4,128,512]{2,1,0:T(8,128)(2,1)S(1)}, bf16[4,256,512]{2,1,0:T(8,128)(2,1)S(1)}, bf16[4,256,512]{2,1,0:T(8,128)(2,1)}, bf16[4,256,512]{2,1,...) custom-call(s32[4]{0:T(128)S(1)} %copy-done.3, s32[4,8]{1,0:T(4,128)S(1)} %copy-done.2, ...), custom_call_target="tpu_custom_call" | custom-call | flops 754974720 | bytes 12582912 | tf_op jit(solution)/shard_map/pallas_call | solution.py:124
  81.0 0.8 copy-done
  81.8 8.3 %collective-permute-start.5 = (bf16[4,256,512]{2,1,0:T(8,128)(2,1)}, bf16[4,256,512]{2,1,0:T(8,128)(2,1)}, u32[]{:S(2)}, u32[]{:S(2)}) collective-permute-start(bf16[4,256,512]{2,1,0:T(8,128)(2,1)} %get-tuple-element.14), channel_id=1, source_target_pairs={{0,1},{1,0},{2,3},{3,2},{4,5},{5,4},{6,7},{7,6},{8,9},{9,8},{10,11... | collective-permute-start | bytes 3145736 | tf_op jit(solution)/shard_map/ppermute | solution.py:24
  90.1 2.6 %collective-permute-done.5 = bf16[4,256,512]{2,1,0:T(8,128)(2,1)} collective-permute-done((bf16[4,256,512]{2,1,0:T(8,128)(2,1)}, bf16[4,256,512]{2,1,0:T(8,128)(2,1)}, u32[]{:S(2)}, u32[]{:S(2)}) %collective-permute-start.5) | collective-permute-done | bytes 1048608 | tf_op jit(solution)/shard_map/ppermute | solution.py:24
  92.7 1.5 add_convert_fusion.2
  94.2 4.3 %collective-permute-start.6 = (bf16[4,256,512]{2,1,0:T(8,128)(2,1)S(1)}, bf16[4,256,512]{2,1,0:T(8,128)(2,1)S(1)}, u32[]{:S(2)}, u32[]{:S(2)}) collective-permute-start(bf16[4,256,512]{2,1,0:T(8,128)(2,1)S(1)} %add_convert_fusion.2), channel_id=1, source_target_pairs={{0,2},{1,3},{2,4},{3,5},{4,6},{5,7},{8,10},{9,11},{10,12},{11,13},... | collective-permute-start | bytes 3145736 | tf_op jit(solution)/shard_map/ppermute | solution.py:19
  98.5 1.5 add_convert_fusion.1
  100.1 1.3 collective-permute-start.7
  101.4 20.0 %collective-permute-done.6 = bf16[4,256,512]{2,1,0:T(8,128)(2,1)S(1)} collective-permute-done((bf16[4,256,512]{2,1,0:T(8,128)(2,1)S(1)}, bf16[4,256,512]{2,1,0:T(8,128)(2,1)S(1)}, u32[]{:S(2)}, u32[]{:S(2)}) %collective-permute-start.6) | collective-permute-done | bytes 1048608 | tf_op jit(solution)/shard_map/ppermute | solution.py:19
  121.4 5.7 %collective-permute-done.7 = bf16[4,256,512]{2,1,0:T(8,128)(2,1)S(1)} collective-permute-done((bf16[4,256,512]{2,1,0:T(8,128)(2,1)S(1)}, bf16[4,256,512]{2,1,0:T(8,128)(2,1)S(1)}, u32[]{:S(2)}, u32[]{:S(2)}) %collective-permute-start.7) | collective-permute-done | bytes 1048608 | tf_op jit(solution)/shard_map/ppermute | solution.py:19
  127.1 2.0 %add_convert_fusion = bf16[4,256,512]{2,1,0:T(8,128)(2,1)S(1)} fusion(bf16[4,256,512]{2,1,0:T(8,128)(2,1)S(1)} %collective-permute-done.7, bf16[4,256,512]{2,1,0:T(8,128)(2,1)S(1)} %collective-permute-done.6, bf16[4,256,512]{2,1,0:T(8,128)(2,1)S(1)} %get-tuple-element.12, bf16[4,256,512]{2,1,0:T(8,128)(2,1)} %collective-permute-done.4, ...), kind=kLoop, calls=%fused_computation | loop fusion | flops 4718592 | bytes 6291457 | tf_op jit(solution)/shard_map/convert_element_type | solution.py:145
  129.1 0.1 pad_maximum_fusion
  129.2 21.9 %all_to_all.15 = bf16[4,384,512]{2,1,0:T(8,128)(2,1)S(1)} all-to-all(bf16[4,384,512]{2,1,0:T(8,128)(2,1)S(1)} %pad_maximum_fusion), channel_id=1, replica_groups=mesh['frame'=4,'seq'=8] {'frame'}, dimensions={0} | all-to-all | bytes 3145728 | tf_op jit(solution)/shard_map/all_to_all | solution.py:146
  151.2 0.8 maximum_bitcast_fusion.2
  152.0 0.7 maximum_bitcast_fusion.5
  152.7 1.0 maximum_bitcast_fusion
  153.7 0.7 maximum_bitcast_fusion.3
  (28 shorter events, 0.2 us)
Async XLA Ops:
  3.2 5.3 %copy-start.7 = (bf16[1,96,2048]{2,1,0:T(8,128)(2,1)S(1)}, bf16[1,96,2048]{2,1,0:T(8,128)(2,1)}, u32[]{:S(2)}) copy-start(bf16[1,96,2048]{2,1,0:T(8,128)(2,1)} %param.17) | copy-start | bytes 1179652
  3.2 5.3 %copy-start.8 = (bf16[1,96,2048]{2,1,0:T(8,128)(2,1)S(1)}, bf16[1,96,2048]{2,1,0:T(8,128)(2,1)}, u32[]{:S(2)}) copy-start(bf16[1,96,2048]{2,1,0:T(8,128)(2,1)} %param.14) | copy-start | bytes 1179652
  3.2 5.3 %copy-start.9 = (bf16[1,32,2048]{2,1,0:T(8,128)(2,1)S(1)}, bf16[1,32,2048]{2,1,0:T(8,128)(2,1)}, u32[]{:S(2)}) copy-start(bf16[1,32,2048]{2,1,0:T(8,128)(2,1)} %param.13) | copy-start | bytes 393220
  3.2 5.3 %copy-start.10 = (bf16[1,32,2048]{2,1,0:T(8,128)(2,1)S(1)}, bf16[1,32,2048]{2,1,0:T(8,128)(2,1)}, u32[]{:S(2)}) copy-start(bf16[1,32,2048]{2,1,0:T(8,128)(2,1)} %param.10) | copy-start | bytes 393220
  3.2 18.9 %all-to-all-start.1 = ((bf16[4,256,512]{2,1,0:T(8,128)(2,1)}), bf16[4,256,512]{2,1,0:T(8,128)(2,1)S(1)}, u32[]{:S(2)}, u32[]{:S(2)}) async-start(bf16[4,256,512]{2,1,0:T(8,128)(2,1)} %pad_maximum_fusion.4), calls=%async_computation.1 | async-start | bytes 2097152 | tf_op jit(solution)/shard_map/all_to_all | solution.py:104
  22.1 12.4 %copy-start.4 = (bf16[4,256,512]{2,1,0:T(8,128)(2,1)}, bf16[4,256,512]{2,1,0:T(8,128)(2,1)S(1)}, u32[]{:S(2)}) copy-start(bf16[4,256,512]{2,1,0:T(8,128)(2,1)S(1)} %all-to-all-done.1.refs_2_) | copy-start | bytes 3145732
  22.1 31.1 %collective-permute-start = (bf16[4,256,512]{2,1,0:T(8,128)(2,1)S(1)}, bf16[4,256,512]{2,1,0:T(8,128)(2,1)S(1)}, u32[]{:S(2)}, u32[]{:S(2)}) collective-permute-start(bf16[4,256,512]{2,1,0:T(8,128)(2,1)S(1)} %all-to-all-done.1.refs_2_), channel_id=1, source_target_pairs={{2,0},{3,1},{4,2},{5,3},{6,4},{7,5},{10,8},{11,9},{12,10},{13,11},... | collective-permute-start | bytes 3145736 | tf_op jit(solution)/shard_map/ppermute | solution.py:19
  23.4 29.8 %collective-permute-start.1 = (bf16[4,256,512]{2,1,0:T(8,128)(2,1)S(1)}, bf16[4,256,512]{2,1,0:T(8,128)(2,1)}, u32[]{:S(2)}, u32[]{:S(2)}) collective-permute-start(bf16[4,256,512]{2,1,0:T(8,128)(2,1)S(1)} %all-to-all-done.1.refs_2_), channel_id=1, source_target_pairs={{1,0},{2,1},{3,2},{4,3},{5,4},{6,5},{7,6},{9,8},{10,9},{11,10},{12... | collective-permute-start | bytes 3145736 | tf_op jit(solution)/shard_map/ppermute | solution.py:19
  24.7 28.5 %collective-permute-start.2 = (bf16[4,256,512]{2,1,0:T(8,128)(2,1)S(1)}, bf16[4,256,512]{2,1,0:T(8,128)(2,1)}, u32[]{:S(2)}, u32[]{:S(2)}) collective-permute-start(bf16[4,256,512]{2,1,0:T(8,128)(2,1)S(1)} %all-to-all-done.1.refs_2_), channel_id=1, source_target_pairs={{0,1},{1,2},{2,3},{3,4},{4,5},{5,6},{6,7},{8,9},{9,10},{10,11},{11... | collective-permute-start | bytes 3145736 | tf_op jit(solution)/shard_map/ppermute | solution.py:19
  28.8 27.1 %collective-permute-start.3 = (bf16[4,256,512]{2,1,0:T(8,128)(2,1)S(1)}, bf16[4,256,512]{2,1,0:T(8,128)(2,1)}, u32[]{:S(2)}, u32[]{:S(2)}) collective-permute-start(bf16[4,256,512]{2,1,0:T(8,128)(2,1)S(1)} %all-to-all-done.1.refs_2_), channel_id=1, source_target_pairs={{0,2},{1,3},{2,4},{3,5},{4,6},{5,7},{8,10},{9,11},{10,12},{11,13},... | collective-permute-start | bytes 3145736 | tf_op jit(solution)/shard_map/ppermute | solution.py:19
  34.5 21.4 %copy-start.2 = (s32[4,8]{1,0:T(4,128)S(1)}, s32[4,8]{1,0:T(4,128)}, u32[]{:S(2)}) copy-start(s32[4,8]{1,0:T(4,128)} %len_ref.1) | copy-start | bytes 388
  34.5 21.4 %copy-start.3 = (s32[4]{0:T(128)S(1)}, s32[4]{0:T(128)}, u32[]{:S(2)}) copy-start(s32[4]{0:T(128)} %match_ref.1) | copy-start | bytes 52
  34.5 18.7 %all-to-all-start = ((bf16[4,256,512]{2,1,0:T(8,128)(2,1)}), bf16[4,256,512]{2,1,0:T(8,128)(2,1)S(1)}, u32[]{:S(2)}, u32[]{:S(2)}) async-start(bf16[4,256,512]{2,1,0:T(8,128)(2,1)} %pad_maximum_fusion.2), calls=%async_computation | async-start | bytes 2097152 | tf_op jit(solution)/shard_map/all_to_all | solution.py:104
  53.2 2.7 %copy-start.5 = (bf16[4,256,512]{2,1,0:T(8,128)(2,1)}, bf16[4,256,512]{2,1,0:T(8,128)(2,1)S(1)}, u32[]{:S(2)}) copy-start(bf16[4,256,512]{2,1,0:T(8,128)(2,1)S(1)} %all-to-all-done.own_ref) | copy-start | bytes 3145732
  53.2 2.7 %copy-start.6 = (bf16[4,256,512]{2,1,0:T(8,128)(2,1)}, bf16[4,256,512]{2,1,0:T(8,128)(2,1)S(1)}, u32[]{:S(2)}) copy-start(bf16[4,256,512]{2,1,0:T(8,128)(2,1)S(1)} %collective-permute-done.refs_0_) | copy-start | bytes 3145732
  81.0 0.8 copy-start
  81.8 10.9 %collective-permute-start.5 = (bf16[4,256,512]{2,1,0:T(8,128)(2,1)}, bf16[4,256,512]{2,1,0:T(8,128)(2,1)}, u32[]{:S(2)}, u32[]{:S(2)}) collective-permute-start(bf16[4,256,512]{2,1,0:T(8,128)(2,1)} %get-tuple-element.14), channel_id=1, source_target_pairs={{0,1},{1,0},{2,3},{3,2},{4,5},{5,4},{6,7},{7,6},{8,9},{9,8},{10,11... | collective-permute-start | bytes 3145736 | tf_op jit(solution)/shard_map/ppermute | solution.py:24
  90.1 8.5 %collective-permute-start.4 = (bf16[4,256,512]{2,1,0:T(8,128)(2,1)}, bf16[4,256,512]{2,1,0:T(8,128)(2,1)}, u32[]{:S(2)}, u32[]{:S(2)}) collective-permute-start(bf16[4,256,512]{2,1,0:T(8,128)(2,1)} %get-tuple-element.13), channel_id=1, source_target_pairs={{0,1},{1,0},{2,3},{3,2},{4,5},{5,4},{6,7},{7,6},{8,9},{9,8},{10,11... | collective-permute-start | bytes 3145736 | tf_op jit(solution)/shard_map/ppermute | solution.py:24
  94.2 27.1 %collective-permute-start.6 = (bf16[4,256,512]{2,1,0:T(8,128)(2,1)S(1)}, bf16[4,256,512]{2,1,0:T(8,128)(2,1)S(1)}, u32[]{:S(2)}, u32[]{:S(2)}) collective-permute-start(bf16[4,256,512]{2,1,0:T(8,128)(2,1)S(1)} %add_convert_fusion.2), channel_id=1, source_target_pairs={{0,2},{1,3},{2,4},{3,5},{4,6},{5,7},{8,10},{9,11},{10,12},{11,13},... | collective-permute-start | bytes 3145736 | tf_op jit(solution)/shard_map/ppermute | solution.py:19
  100.1 27.0 %collective-permute-start.7 = (bf16[4,256,512]{2,1,0:T(8,128)(2,1)S(1)}, bf16[4,256,512]{2,1,0:T(8,128)(2,1)S(1)}, u32[]{:S(2)}, u32[]{:S(2)}) collective-permute-start(bf16[4,256,512]{2,1,0:T(8,128)(2,1)S(1)} %add_convert_fusion.1), channel_id=1, source_target_pairs={{2,0},{3,1},{4,2},{5,3},{6,4},{7,5},{10,8},{11,9},{12,10},{13,11},... | collective-permute-start | bytes 3145736 | tf_op jit(solution)/shard_map/ppermute | solution.py:19
  127.1 2.0 %copy-start.1 = (bf16[4,128,512]{2,1,0:T(8,128)(2,1)S(1)}, bf16[4,128,512]{2,1,0:T(8,128)(2,1)}, u32[]{:S(2)}) copy-start(bf16[4,128,512]{2,1,0:T(8,128)(2,1)} %copy-done) | copy-start | bytes 1572868
